TPU v7x, 128 devices: a whole 4x4x4 slice. The times are simulated.
128 devices in a mesh: dp: 4 (over y), lists: 32 (over z, x, core).
Axes of the slice: x: 4, y: 4, z: 4, core: 2. Of those that a mesh axis runs over, the one named last changes fastest.
Arguments:
- embeddings: bfloat16 [131072, 1024], P('dp', 'lists'), may hold values from -6 to 6
- assign: int32 [131072], P(('dp', 'lists')), may hold values from 0 to 65535, as said below
- list_slot: int32 [65536], replicated, may hold values from 0 to 65535, as said below
- centroids: bfloat16 [65536, 1024], P('lists'), may hold values from -3 to 3
- rotation: bfloat16 [32, 1024, 1024], P('lists'), may hold values from -0.1875 to 0.1875
- codebook: bfloat16 [16, 256, 64], replicated, may hold values from -6 to 6
Outputs:
- quant_error: float32 [16, 131072], P(None, ('dp', 'lists'))
Inputs may be any that keep to these rules, and one draw needn't show every extreme that they name: A permutation of the lists; list l belongs to the group list_slot[l] // 2048. `assign`: among the 1024 vectors of one device (aligned blocks in order), at most 96 belong to the lists of any one group, and one group, the same for every device, gets exactly 96 from each device.
All inputs are finite; a program needn't handle non-finite values.
Results may differ from a plain program's by a relative error of at most 0.0016.
Values may be sent and summed in bfloat16 or wider, within the bound.
A program may use at most 128 MiB of HBM per device.

v0:
```python
import jax
import jax.numpy as jnp
from jax import lax
from jax.sharding import PartitionSpec as P


def route_rows(assigned, list_slot, list_width, owner_count):
    slot_index = jnp.take(list_slot, assigned)
    target = slot_index // list_width
    local_row = slot_index - target * list_width
    onehot = (target[..., None] == jnp.arange(owner_count, dtype=jnp.int32)).astype(jnp.int32)
    position = jnp.sum(jnp.cumsum(onehot, axis=-2) * onehot, axis=-1) - 1
    return (target, local_row, position)


def encode_rows(received, row_ids, centroids, rotation, codebook, code_norms):
    senders, slot_count, model_width = received.shape
    flattened = received.reshape(senders * slot_count, model_width)
    centre_rows = jnp.take(centroids, row_ids.reshape(-1), axis=0)
    residual = (flattened.astype(jnp.float32) - centre_rows.astype(jnp.float32)).astype(
        jnp.bfloat16
    )
    rotated = jnp.dot(residual, rotation[0], preferred_element_type=jnp.float32).astype(
        jnp.bfloat16
    )
    book_count, centres, sub_width = codebook.shape

    def one_book(book_index):
        subspace = lax.dynamic_slice_in_dim(rotated, book_index * sub_width, sub_width, 1)
        codewords = lax.dynamic_index_in_dim(codebook, book_index, 0, keepdims=False)
        norm_row = lax.dynamic_index_in_dim(code_norms, book_index, 0, keepdims=False)
        products = lax.dot_general(
            subspace, codewords, (((1,), (1,)), ((), ())), preferred_element_type=jnp.float32
        )
        lengths = jnp.sum(jnp.square(subspace.astype(jnp.float32)), axis=1)
        distance = lengths[:, None] + norm_row[None, :] - 2.0 * products
        return jnp.min(distance, axis=1) / sub_width

    errors = lax.map(one_book, jnp.arange(book_count, dtype=jnp.int32))
    errors = errors.reshape(book_count, senders, slot_count).transpose(1, 0, 2)
    return lax.all_to_all(errors, "lists", split_axis=0, concat_axis=0, tiled=True)


def shards(embeddings, assign, list_slot, centroids, rotation, codebook):
    owner_count = lax.axis_size("lists")
    list_width = centroids.shape[0]
    home_rows = assign.shape[0]
    capacity = 3 * home_rows // owner_count
    model_width = rotation.shape[1]
    code_norms = jnp.sum(jnp.square(codebook.astype(jnp.float32)), axis=2)
    target, local_row, position = route_rows(assign, list_slot, list_width, owner_count)
    vectors = lax.all_to_all(embeddings, "lists", split_axis=0, concat_axis=1, tiled=True)
    outgoing = (
        jnp.zeros((owner_count, capacity, model_width), jnp.bfloat16)
        .at[target, position]
        .set(vectors)
    )
    row_ids = jnp.zeros((owner_count, capacity), jnp.int32).at[target, position].set(local_row)
    returned = encode_rows(
        lax.all_to_all(outgoing, "lists", split_axis=0, concat_axis=0, tiled=True),
        lax.all_to_all(row_ids, "lists", split_axis=0, concat_axis=0, tiled=True),
        centroids,
        rotation,
        codebook,
        code_norms,
    )
    return jnp.transpose(returned, (1, 0, 2))[:, target, position]


def solution(mesh):
    placed = (
        P("dp", "lists"),
        P(("dp", "lists")),
        P(),
        P("lists", None),
        P("lists", None, None),
        P(),
    )
    return jax.shard_map(
        shards, mesh=mesh, in_specs=placed, out_specs=P(None, ("dp", "lists")), check_vma=False
    )
```

profile of v0, /device:TPU:1, one launch (start us, length us, event | category | flops | bytes accessed | tf_op | source)
XLA Modules:
  0.0 298.1 jit_solution(8096517613341768460)
XLA Ops:
  0.0 3.3 %copy.36 = bf16[4,32,8,1024]{3,2,0,1:T(8,128)(2,1)} copy(bf16[4,32,8,1024]{3,2,1,0:T(8,128)(2,1)} %bitcast.58) | data formatting | bytes 4194304 | tf_op jit(solution)/shard_map/all_to_all | solution.py:52
  3.3 9.5 %all-to-all-start = ((bf16[32,1024,32]{1,2,0:T(8,128)(2,1)}), bf16[32,1024,32]{1,2,0:T(8,128)(2,1)}, u32[]{:S(2)}, u32[]{:S(2)}) async-start(bf16[32,1024,32]{1,2,0:T(8,128)(2,1)} %bitcast.55), calls=%async_computation | async-start | bytes 4194304 | tf_op jit(solution)/shard_map/all_to_all | solution.py:52
  12.8 6.2 %gather_fusion = s32[1024]{0:T(1024)S(1)} fusion(s32[65536]{0:T(1024)S(1)} %copy-done.1, s32[1024]{0:T(1024)S(1)} %fusion.16), kind=kCustom, calls=%fused_computation | custom fusion | bytes 12288 | tf_op jit(solution)/shard_map/jit(_take)/gather | solution.py:8
  19.0 9.0 %reduce-window.6 = s32[32,8,128]{2,1,0:T(8,128)S(1)} reduce-window(s32[32,8,128]{2,1,0:T(8,128)S(1)} %fusion.11, s32[]{:T(128)} %constant.81.clone.1), window={size=1x1x128 pad=0_0x0_0x127_0}, to_apply=%region_0.0 | reduce-window | flops 4161536 | bytes 262148 | tf_op jit(solution)/shard_map/reduce-window
  28.8 4.3 %scatter_custom_fusion.1 = s32[3072]{0:T(1024)S(1)} fusion(s32[1024]{0:T(1024)S(1)} %broadcast_select_fusion, s32[1024]{0:T(1024)S(1)} %get-tuple-element.52, s32[]{:T(128)} %constant.81.clone.1), kind=kCustom, calls=%fused_computation.39 | custom fusion | bytes 12292
  33.2 0.7 all_to_all.31
  33.8 6.9 %all-to-all-done = bf16[32,1024,32]{1,2,0:T(8,128)(2,1)} async-done(((bf16[32,1024,32]{1,2,0:T(8,128)(2,1)}), bf16[32,1024,32]{1,2,0:T(8,128)(2,1)}, u32[]{:S(2)}, u32[]{:S(2)}) %all-to-all-start) | async-done | bytes 2097184 | tf_op jit(solution)/shard_map/all_to_all | solution.py:52
  40.7 5.9 %all-to-all-start.2 = ((s32[32,1,96]{2,1,0:T(1,128)}), s32[32,1,96]{2,1,0:T(1,128)S(1)}, u32[]{:S(2)}, u32[]{:S(2)}) async-start(s32[32,1,96]{2,1,0:T(1,128)} %all_to_all.31), calls=%async_computation.2 | async-start | bytes 32768 | tf_op jit(solution)/shard_map/all_to_all | solution.py:61
  46.6 4.0 %copy.28 = bf16[1024,1024]{1,0:T(8,128)(2,1)} copy(bf16[1024,1024]{0,1:T(8,128)(2,1)} %bitcast.11) | data formatting | bytes 4194304 | tf_op jit(solution)/shard_map/all_to_all | solution.py:52
  50.5 9.8 %scatter_custom_fusion = bf16[3072,1024]{1,0:T(8,128)(2,1)} fusion(s32[1024]{0:T(1024)S(1)} %broadcast_select_fusion, bf16[1024,1024]{1,0:T(8,128)(2,1)} %copy.28, bf16[]{:T(256)} %constant.83.clone.1), kind=kCustom, calls=%fused_computation.17 | custom fusion | bytes 6291968
  60.3 7.7 %all-to-all-start.1 = ((bf16[32,96,1024]{2,1,0:T(8,128)(2,1)}), bf16[32,96,1024]{2,1,0:T(8,128)(2,1)}, u32[]{:S(2)}, u32[]{:S(2)}) async-start(bf16[32,96,1024]{2,1,0:T(8,128)(2,1)} %bitcast.53), calls=%async_computation.1 | async-start | bytes 12582912 | tf_op jit(solution)/shard_map/all_to_all | solution.py:60
  68.7 0.6 reduce.9
  69.5 18.6 %gather_fusion.1 = bf16[3072,1024]{1,0:T(8,128)(2,1)} fusion(bf16[2048,1024]{1,0:T(8,128)(2,1)} %param.11, s32[3072]{0:T(1024)S(1)} %broadcast_clamp_fusion), kind=kCustom, calls=%fused_computation.1 | custom fusion | bytes 12595200 | tf_op jit(solution)/shard_map/jit(_take)/gather | solution.py:19
  88.1 52.8 %all-to-all-done.1 = bf16[32,96,1024]{2,1,0:T(8,128)(2,1)} async-done(((bf16[32,96,1024]{2,1,0:T(8,128)(2,1)}), bf16[32,96,1024]{2,1,0:T(8,128)(2,1)}, u32[]{:S(2)}, u32[]{:S(2)}) %all-to-all-start.1) | async-done | bytes 6291488 | tf_op jit(solution)/shard_map/all_to_all | solution.py:60
  140.9 6.0 %subtract_convert_fusion = bf16[32,96,1024]{2,1,0:T(8,128)(2,1)S(1)} fusion(bf16[32,96,1024]{2,1,0:T(8,128)(2,1)} %all-to-all-done.1, bf16[32,96,1024]{2,1,0:T(8,128)(2,1)} %bitcast.54, pred[32,96]{1,0:T(8,128)(4,1)S(1)} %compare_and_fusion), kind=kLoop, calls=%fused_computation.15 | loop fusion | flops 15728640 | bytes 18877440 | tf_op jit(solution)/shard_map/convert_element_type | solution.py:20
  147.0 8.7 %convolution_convert_fusion = bf16[3072,1024]{1,0:T(8,128)(2,1)} fusion(bf16[3072,1024]{1,0:T(8,128)(2,1)S(1)} %bitcast.56, bf16[1,1024,1024]{2,1,0:T(8,128)(2,1)S(1)} %copy-done), kind=kOutput, calls=%fused_computation.16 | convolution fusion | flops 6445596672 | bytes 14680064 | tf_op jit(solution)/shard_map/dot_general | solution.py:23
  155.7 112.4 %while.10 = (s32[]{:T(128)}, f32[16,3072]{1,0:T(8,128)S(1)}, s32[16]{0:T(128)S(1)}, bf16[3072,1024]{1,0:T(8,128)(2,1)}, f32[16,256]{1,0:T(8,128)S(1)}, /*index=5...) while((s32[]{:T(128)}, f32[16,3072]{1,0:T(8,128)S(1)}, ...), condition=%wide.region_9.10_spmd, body=%wide.region_6.9_spmd.sunk | while | flops 104395784 | bytes 1301725 | solution.py:39
  156.8 1.8 multiply_reduce_fusion.4
  160.4 1.9 fusion.23
  163.9 1.8 multiply_reduce_fusion.4
  167.5 1.9 fusion.23
  169.7 0.6 dynamic_slice.32
  170.9 1.8 multiply_reduce_fusion.4
  174.5 1.9 fusion.23
  176.7 0.6 dynamic_slice.32
  177.9 1.8 multiply_reduce_fusion.4
  181.5 1.9 fusion.23
  183.8 0.6 dynamic_slice.32
  184.9 1.8 multiply_reduce_fusion.4
  188.5 1.9 fusion.23
  190.8 0.6 dynamic_slice.32
  192.0 1.8 multiply_reduce_fusion.4
  195.6 1.9 fusion.23
  197.8 0.6 dynamic_slice.32
  199.0 1.8 multiply_reduce_fusion.4
  202.6 1.9 fusion.23
  204.8 0.6 dynamic_slice.32
  206.0 1.8 multiply_reduce_fusion.4
  209.6 1.9 fusion.23
  211.9 0.6 dynamic_slice.32
  213.0 1.8 multiply_reduce_fusion.4
  216.6 1.9 fusion.23
  218.9 0.6 dynamic_slice.32
  220.1 1.8 multiply_reduce_fusion.4
  223.6 1.9 fusion.23
  227.1 1.8 multiply_reduce_fusion.4
  230.7 1.9 fusion.23
  234.1 1.8 multiply_reduce_fusion.4
  237.7 1.9 fusion.23
  241.1 1.8 multiply_reduce_fusion.4
  244.7 1.9 fusion.23
  247.0 0.6 dynamic_slice.32
  248.2 1.8 multiply_reduce_fusion.4
  251.7 1.9 fusion.23
  254.0 0.6 dynamic_slice.32
  255.2 1.8 multiply_reduce_fusion.4
  258.8 1.9 fusion.23
  261.0 0.6 dynamic_slice.32
  262.2 1.8 multiply_reduce_fusion.4
  265.8 1.9 fusion.23
  268.3 16.9 %all_to_all.38 = f32[32,16,96]{2,1,0:T(8,128)S(1)} all-to-all(f32[32,16,96]{2,1,0:T(8,128)S(1)} %copy.29), channel_id=1, replica_groups=mesh['dp'=4,'lists'=32] {'lists'}, dimensions={0} | all-to-all | bytes 393216 | tf_op jit(solution)/shard_map/all_to_all | solution.py:41
  285.2 1.6 copy.30
  286.8 10.5 %gather_fusion.2 = f32[1024,16]{1,0:T(8,128)S(1)} fusion(f32[16,32,96]{0,2,1:T(8,128)} %bitcast.57, s32[1024]{0:T(1024)S(1)} %bitcast.52), kind=kCustom, calls=%fused_computation.2 | custom fusion | bytes 139264 | tf_op jit(solution)/shard_map/gather | solution.py:67
  297.3 0.8 copy.31
  (92 shorter events, 9.7 us)
Async XLA Ops:
  0.0 147.0 %copy-start = (bf16[1,1024,1024]{2,1,0:T(8,128)(2,1)S(1)}, bf16[1,1024,1024]{2,1,0:T(8,128)(2,1)}, u32[]{:S(2)}) copy-start(bf16[1,1024,1024]{2,1,0:T(8,128)(2,1)} %param.12) | copy-start | bytes 6291460
  0.0 12.8 %copy-start.3 = (s32[1024]{0:T(1024)S(1)}, s32[1024]{0:T(1024)}, u32[]{:S(2)}) copy-start(s32[1024]{0:T(1024)} %param.9) | copy-start | bytes 12292
  0.0 12.8 %copy-start.1 = (s32[65536]{0:T(1024)S(1)}, s32[65536]{0:T(1024)}, u32[]{:S(2)}) copy-start(s32[65536]{0:T(1024)} %param.10) | copy-start | bytes 786436
  0.0 28.6 %copy-start.5 = (s32[2]{0:T(128)S(1)}, s32[2]{0:T(128)}, u32[]{:S(2)}) copy-start(s32[2]{0:T(128)} %constant.96) | copy-start | bytes 28
  0.0 28.7 %copy-start.4 = (s32[2]{0:T(128)S(1)}, s32[2]{0:T(128)}, u32[]{:S(2)}) copy-start(s32[2]{0:T(128)} %constant.99) | copy-start | bytes 28
  3.3 37.4 %all-to-all-start = ((bf16[32,1024,32]{1,2,0:T(8,128)(2,1)}), bf16[32,1024,32]{1,2,0:T(8,128)(2,1)}, u32[]{:S(2)}, u32[]{:S(2)}) async-start(bf16[32,1024,32]{1,2,0:T(8,128)(2,1)} %bitcast.55), calls=%async_computation | async-start | bytes 4194304 | tf_op jit(solution)/shard_map/all_to_all | solution.py:52
  40.7 19.6 %all-to-all-start.2 = ((s32[32,1,96]{2,1,0:T(1,128)}), s32[32,1,96]{2,1,0:T(1,128)S(1)}, u32[]{:S(2)}, u32[]{:S(2)}) async-start(s32[32,1,96]{2,1,0:T(1,128)} %all_to_all.31), calls=%async_computation.2 | async-start | bytes 32768 | tf_op jit(solution)/shard_map/all_to_all | solution.py:61
  60.3 7.7 %copy-start.2 = (bf16[16,256,64]{1,2,0:T(8,128)(2,1)S(1)}, bf16[16,256,64]{1,2,0:T(8,128)(2,1)}, u32[]{:S(2)}) copy-start(bf16[16,256,64]{1,2,0:T(8,128)(2,1)} %param.13) | copy-start | bytes 1572868
  60.3 80.6 %all-to-all-start.1 = ((bf16[32,96,1024]{2,1,0:T(8,128)(2,1)}), bf16[32,96,1024]{2,1,0:T(8,128)(2,1)}, u32[]{:S(2)}, u32[]{:S(2)}) async-start(bf16[32,96,1024]{2,1,0:T(8,128)(2,1)} %bitcast.53), calls=%async_computation.1 | async-start | bytes 12582912 | tf_op jit(solution)/shard_map/all_to_all | solution.py:60
where the time goes:
time: 301 us; the launch traced here: 298 us
  local copies, waits for them, and re-layouts  75.3 us (25%)
  waiting for transfers between devices  59.7 us (20%)
  other arithmetic  45.7 us (15%)
  matrix products  39.5 us (13%)
  loops' own time  37.7 us (13%)
  starting transfers between devices  23 us (8%)
  blocking collectives  16.9 us (6%)
    all_to_all x1, waiting for transfers between devices, shards(): lax.all_to_all(outgoing, 'lists', split_axis=0, concat_axis=0, tiled=True)  52.8 us
    another operation x1, loops' own time, encode_rows(): errors = lax.map(one_book, jnp.arange(book_count, dtype=jnp.int32))  37.7 us
    dot_general x16, matrix products, one_book(): lax.dot_general(subspace, codewords, (((1,), (1,)), ((), ())), preferred_...  30.8 us
    reduce_sum x16, other arithmetic, one_book(): lengths = jnp.sum(jnp.square(subspace.astype(jnp.float32)), axis=1)  29.4 us
    gather x1, local copies, waits for them, and re-layouts, encode_rows(): centre_rows = jnp.take(centroids, row_ids.reshape(-1), axis=0)  18.6 us
    all_to_all x1, blocking collectives, encode_rows(): lax.all_to_all(errors, 'lists', split_axis=0, concat_axis=0, tiled=True)  16.9 us
    unnamed x14, local copies, waits for them, and re-layouts  14.1 us
    gather x2, local copies, waits for them, and re-layouts, shards(): return jnp.transpose(returned, (1, 0, 2))[:, target, position]  11.3 us
  transfers between devices with their start and end apart: 3, of which 2 were waited for; matrix products, arithmetic and copies ran while one was open for 18% of the time, Pallas kernels for 0%

commit v1 on v0

v1 whole, which is shorter than its diff:
```python
import functools

import jax
import jax.numpy as jnp
from jax import lax
from jax.experimental import pallas as pl
from jax.experimental.pallas import tpu as pltpu
from jax.sharding import PartitionSpec as P

MESH = pl.DeviceIdType.MESH
F32 = jnp.float32
BF16 = jnp.bfloat16
I32 = jnp.int32

N = 32
CAP = 96
HOME = 1024
D = 1024
FS = 32
LISTS = 2048
BOOKS, CODES, SUB = 16, 256, 64
CHUNKS = 4
CH = N * CAP // CHUNKS
QUAD = 4 * CAP


def dot(a, b):
    return jnp.dot(a, b, preferred_element_type=F32)


def iota(shape, dim):
    return lax.broadcasted_iota(I32, shape, dim)


def routes(assign_ref, slots_ref):
    assigned = assign_ref[...]
    table = slots_ref[...].astype(F32).T.astype(I32)
    table = jnp.concatenate([table >> 8, table & 255], axis=0).astype(F32).astype(BF16)
    rows = (iota((512, HOME), 0) == (assigned >> 7)).astype(F32).astype(BF16)
    picked = dot(table, rows)
    low = iota((128, HOME), 0) == (assigned & 127)
    upper = jnp.sum(jnp.where(low, picked[:128], 0.0), axis=0, keepdims=True)
    lower = jnp.sum(jnp.where(low, picked[128:], 0.0), axis=0, keepdims=True)
    slot = upper.astype(I32) * 256 + lower.astype(I32)
    target, local = slot >> 11, slot & (LISTS - 1)
    mine = iota((N, HOME), 0) == target
    onehot = mine.astype(F32)
    before = (iota((HOME, HOME), 0) < iota((HOME, HOME), 1)).astype(F32).astype(BF16)
    ahead = dot(onehot.astype(BF16), before)
    position = jnp.sum(jnp.where(mine, ahead, 0.0), axis=0, keepdims=True).astype(I32)
    place = (iota((128, HOME), 0) == position).astype(F32).astype(BF16)
    vector = iota((1, HOME), 1)
    fields = [vector & 255, vector >> 8, local & 255, local >> 8]
    planes = [jnp.where(mine, field.astype(F32), 0.0) for field in fields] + [onehot]
    planes = jnp.concatenate(planes, axis=0).astype(BF16)
    held = lax.dot_general(planes, place, (((1,), (1,)), ((), ())), preferred_element_type=F32).astype(I32)
    index, group, local_low, local_high, valid = (held[N * j : N * (j + 1)] for j in range(5))
    group = jnp.where(valid > 0, group, 32)
    entry = index + (group << 8) + (local_low << 14) + (local_high << 22)
    return target * 128 + position, entry


def kernel(
    emb_ref, assign_ref, slots_ref, cent_ref, rot_ref, book_ref, out_ref,
    xb, send, recv, near, cent, cent_t, rot, rot_t, codes, tab_own, tab_all, tab, resid, sub, errs,
    code_ref, ret_send, ret_recv,
    x_sem, c_sem, r_sem, tab_ss, tab_rs, vec_ss, vec_rs, ret_ss, ret_rs,
):
    me = lax.axis_index("lists")

    def peer(k):
        return lax.rem(me + k, N)

    barrier = pltpu.get_barrier_semaphore()

    @pl.loop(1, N)
    def _(k):
        pl.semaphore_signal(barrier, inc=1, device_id={"lists": peer(k)}, device_id_type=MESH)

    def x_copy(t):
        block = t // 8
        group = t - block * 8
        return pltpu.make_async_copy(
            emb_ref.at[:, pl.ds(pl.multiple_of(t * 256, 256), 256)],
            xb.at[block, pl.ds(pl.multiple_of(group * FS, FS), FS), :],
            x_sem.at[t],
        )

    @pl.loop(0, 128)
    def _(t):
        x_copy(t).start()

    c_copy = pltpu.make_async_copy(cent_ref, cent, c_sem)
    r_copy = pltpu.make_async_copy(rot_ref, rot, r_sem)
    c_copy.start()
    r_copy.start()

    code, entry = routes(assign_ref, slots_ref)
    code_ref[...] = code
    tab_own[...] = entry

    pl.semaphore_wait(barrier, N - 1)

    def tab_copy(k, home):
        return pltpu.make_async_remote_copy(
            src_ref=tab_own,
            dst_ref=tab_all.at[home],
            send_sem=tab_ss.at[k],
            recv_sem=tab_rs.at[k],
            device_id={"lists": peer(k)},
            device_id_type=MESH,
        )

    @pl.loop(1, N)
    def _(k):
        tab_copy(k, me).start()

    tab_all[me] = entry

    @pl.loop(0, 128)
    def _(t):
        x_copy(t).wait()

    @pl.loop(1, N)
    def _(k):
        tab_copy(k, lax.rem(me + N - k, N)).wait_recv()

    lane = iota((N, 128), 1)

    @pl.loop(0, N // 4)
    def _(q):
        parts = [tab_all[4 * q + j] + (j << 10) for j in range(4)]
        rolled = [parts[0]] + [pltpu.roll(parts[j], 128 - 32 * j, 1) for j in range(1, 4)]
        base = pl.multiple_of(q * QUAD, 128)
        for j in range(3):
            tab[:, pl.ds(base + 128 * j, 128)] = jnp.where(lane < 96 - 32 * j, rolled[j], rolled[j + 1])

    def select(owner, q):
        entries = tab[pl.ds(owner, 1), pl.ds(pl.multiple_of(q * QUAD, 128), QUAD)]
        index, group = entries & 255, (entries >> 8) & 63
        onehot = (iota((256, QUAD), 0) == index).astype(F32).astype(BF16)
        halves = []
        for half in range(2):
            lanes = slice(128 * half, 128 * half + 256)
            every = dot(xb[2 * q + half], onehot[:, lanes])
            groups = jnp.broadcast_to(group[:, lanes], (FS, 256))
            kept = jnp.zeros((FS, 256), F32)
            for g in range(8):
                kept = jnp.where(groups == g + 8 * half, every[FS * g : FS * (g + 1)], kept)
            halves.append(kept)
        left, right = halves
        return jnp.concatenate([left[:, :128], left[:, 128:] + right[:, :128], right[:, 128:]], axis=1).astype(BF16)

    def vec_copy(c, k, slice_of):
        return pltpu.make_async_remote_copy(
            src_ref=send.at[c, k],
            dst_ref=recv.at[c, pl.ds(pl.multiple_of(slice_of * FS, FS), FS), :],
            send_sem=vec_ss.at[c, k],
            recv_sem=vec_rs.at[c, k],
            device_id={"lists": peer(k)},
            device_id_type=MESH,
        )

    @pl.loop(0, CHUNKS)
    def _(c):
        @pl.loop(1, N)
        def _(k):
            for j in range(2):
                send[c, k, :, QUAD * j : QUAD * (j + 1)] = select(peer(k), 2 * c + j)
            vec_copy(c, k, me).start()

        for j in range(2):
            recv[c, pl.ds(pl.multiple_of(me * FS, FS), FS), QUAD * j : QUAD * (j + 1)] = select(me, 2 * c + j)

    c_copy.wait()
    r_copy.wait()

    @pl.loop(0, 4)
    def _(i):
        @pl.loop(0, 4)
        def _(j):
            rows, columns = pl.multiple_of(i * 256, 256), pl.multiple_of(j * 256, 256)
            rot_t[pl.ds(columns, 256), pl.ds(rows, 256)] = rot[pl.ds(rows, 256), pl.ds(columns, 256)].T

    @pl.loop(0, 8)
    def _(i):
        @pl.loop(0, 4)
        def _(j):
            rows, columns = pl.multiple_of(i * 256, 256), pl.multiple_of(j * 256, 256)
            cent_t[pl.ds(columns, 256), pl.ds(rows, 256)] = cent[pl.ds(rows, 256), pl.ds(columns, 256)].T

    @pl.loop(0, BOOKS)
    def _(m):
        words = book_ref[m].astype(F32)
        norm = jnp.sum(words * words, axis=0, keepdims=True)
        first = norm.astype(BF16).astype(F32)
        second = (norm - first).astype(BF16).astype(F32)
        third = norm - first - second
        row = iota((SUB, CODES), 0)
        extra = jnp.where(row == 0, first, jnp.where(row == 1, second, jnp.where(row == 2, third, 0.0)))
        codes[m] = jnp.concatenate([words * -2.0, extra], axis=0).T.astype(BF16)

    sub[:, SUB:, :] = jnp.ones((4, SUB, CH), BF16)

    @pl.loop(0, N * CAP // 256)
    def _(t):
        lanes = pl.ds(pl.multiple_of(t * 256, 256), 256)
        local = tab[pl.ds(me, 1), lanes] >> 14
        onehot = (iota((LISTS, 256), 0) == local).astype(F32).astype(BF16)

        @pl.loop(0, 4)
        def _(i):
            rows = pl.ds(pl.multiple_of(i * 256, 256), 256)
            near[rows, lanes] = dot(cent_t[rows, :], onehot).astype(BF16)

    def ret_copy(home, owner):
        return pltpu.make_async_remote_copy(
            src_ref=ret_send.at[home],
            dst_ref=ret_recv.at[owner],
            send_sem=ret_ss.at[home],
            recv_sem=ret_rs.at[owner],
            device_id={"lists": home},
            device_id_type=MESH,
        )

    wide = iota((BOOKS, 128), 1)

    @pl.loop(0, CHUNKS)
    def _(c):
        @pl.loop(1, N)
        def _(k):
            vec_copy(c, k, lax.rem(me + N - k, N)).wait_recv()

        lanes = pl.ds(pl.multiple_of(c * CH, 256), CH)

        @pl.loop(0, 4)
        def _(i):
            rows = pl.ds(pl.multiple_of(i * 256, 256), 256)
            resid[rows, :] = (recv[c, rows, :].astype(F32) - near[rows, lanes].astype(F32)).astype(BF16)

        @pl.loop(0, 4)
        def _(i):
            rows = pl.ds(pl.multiple_of(i * 256, 256), 256)
            turned = dot(rot_t[rows, :], resid[...]).astype(BF16)
            for j in range(4):
                piece = turned[SUB * j : SUB * (j + 1)]
                sub[j, :SUB, :] = piece
                squares = piece.astype(F32)
                length = jnp.sum(squares * squares, axis=0, keepdims=True)
                least = jnp.min(dot(codes[4 * i + j], sub[j]), axis=0, keepdims=True)
                errs[pl.ds(4 * i + j, 1), :] = (length + least) * (1.0 / SUB)

        for q in range(2):
            tiles = [errs[:, QUAD * q + 128 * j : QUAD * q + 128 * (j + 1)] for j in range(3)]
            pieces = [
                tiles[0],
                pltpu.roll(jnp.where(wide < 64, tiles[1], tiles[0]), 32, 1),
                pltpu.roll(jnp.where(wide < 32, tiles[2], tiles[1]), 64, 1),
                pltpu.roll(tiles[2], 96, 1),
            ]
            for j in range(4):
                home = 8 * c + 4 * q + j
                piece = jnp.where(wide < CAP, pieces[j], 0.0)
                ret_send[home] = piece

                @pl.when(home == me)
                def _():
                    ret_recv[home] = piece

                @pl.when(home != me)
                def _():
                    ret_copy(home, me).start()

    @pl.loop(1, N)
    def _(k):
        ret_copy(me, peer(k)).wait_recv()

    def spread(t, total):
        got = jnp.concatenate([ret_recv[2 * t], ret_recv[2 * t + 1]], axis=1)
        high = got.astype(BF16)
        low = (got - high.astype(F32)).astype(BF16)
        onehot = (iota((256, HOME), 0) + 256 * t == code_ref[...]).astype(F32).astype(BF16)
        return total + dot(jnp.concatenate([high, low], axis=0), onehot)

    total = lax.fori_loop(0, N // 2, spread, jnp.zeros((2 * BOOKS, HOME), F32))
    out_ref[...] = total[:BOOKS] + total[BOOKS:]

    @pl.loop(1, N)
    def _(k):
        tab_copy(k, me).wait_send()
        ret_copy(peer(k), me).wait_send()

        @pl.loop(0, CHUNKS)
        def _(c):
            vec_copy(c, k, me).wait_send()


def shards(embeddings, assign, list_slot, centroids, rotation, codebook):
    vmem = pl.BlockSpec(memory_space=pltpu.VMEM)
    hbm = pl.BlockSpec(memory_space=pl.ANY)
    dma = pltpu.SemaphoreType.DMA
    return pl.pallas_call(
        kernel,
        out_shape=jax.ShapeDtypeStruct((BOOKS, HOME), F32),
        in_specs=[hbm, vmem, vmem, hbm, hbm, vmem],
        out_specs=vmem,
        scratch_shapes=[
            pltpu.VMEM((16, 256, 256), BF16),
            pltpu.VMEM((CHUNKS, N, FS, CH), BF16),
            pltpu.VMEM((CHUNKS, D, CH), BF16),
            pltpu.VMEM((D, N * CAP), BF16),
            pltpu.VMEM((LISTS, D), BF16),
            pltpu.VMEM((D, LISTS), BF16),
            pltpu.VMEM((D, D), BF16),
            pltpu.VMEM((D, D), BF16),
            pltpu.VMEM((BOOKS, CODES, 2 * SUB), BF16),
            pltpu.VMEM((N, 128), I32),
            pltpu.VMEM((N, N, 128), I32),
            pltpu.VMEM((N, N * CAP), I32),
            pltpu.VMEM((D, CH), BF16),
            pltpu.VMEM((4, 2 * SUB, CH), BF16),
            pltpu.VMEM((BOOKS, CH), F32),
            pltpu.VMEM((1, HOME), I32),
            pltpu.VMEM((N, BOOKS, 128), F32),
            pltpu.VMEM((N, BOOKS, 128), F32),
            dma((128,)), dma, dma,
            dma((N,)), dma((N,)),
            dma((CHUNKS, N)), dma((CHUNKS, N)),
            dma((N,)), dma((N,)),
        ],
        compiler_params=pltpu.CompilerParams(
            collective_id=0, has_side_effects=True, vmem_limit_bytes=58 * 2**20
        ),
        name="encode",
    )(
        embeddings.T,
        assign.reshape(1, HOME),
        list_slot.reshape(512, 128),
        centroids,
        rotation.reshape(D, D),
        codebook.transpose(0, 2, 1),
    )


def solution(mesh):
    placed = (
        P("dp", "lists"),
        P(("dp", "lists")),
        P(),
        P("lists", None),
        P("lists", None, None),
        P(),
    )
    return jax.shard_map(
        shards, mesh=mesh, in_specs=placed, out_specs=P(None, ("dp", "lists")), check_vma=False
    )
```

time: 301 us -> 125 us (0.42)
  the two profiles are of different devices: /device:TPU:1 before, /device:TPU:97 now
where the time goes in v1:
time: 125 us
  Pallas kernels  123 us (98%)
  local copies, waits for them, and re-layouts  1.47 us (1%)
    pallas_call x1, Pallas kernels, shards(): pl.pallas_call(kernel, out_shape=jax.ShapeDtypeStruct((BOOKS, HOME), F32)...  123 us

profile of v1, /device:TPU:97, one launch (start us, length us, event | category | flops | bytes accessed | tf_op | source)
XLA Modules:
  0.0 124.9 jit_solution(9426268429801214079)
XLA Ops:
  0.0 123.5 %encode.1 = f32[16,1024]{1,0:T(8,128)} custom-call(bf16[32,32768]{1,0:T(8,128)(2,1)} %bitcast.5, s32[1,1024]{1,0:T(1,128)} %bitcast.9, s32[512,128]{1,0:T(8,128)} %bitcast.8, bf16[2048,1024]{1,0:T(8,128)(2,1)} %cent_ref.1, bf16[1024,1024]{1,0:T(8,128)(2,1)} %bitcast.6, bf16[16,64,256]{2,1,0:T(8,128)(2,1)} %bitcast.7), custom_call_target="tpu_custom_call" | custom-call | tf_op jit(solution)/shard_map/encode/pallas_call | solution.py:302
  123.5 1.5 %copy.8 = f32[16,1024]{1,0:T(8,128)} copy(f32[16,1024]{1,0:T(8,128)} %encode.1) | data formatting | bytes 131072

commit v2 on v0

--- a/solution.py
+++ b/solution.py
@@ -1,7 +1,511 @@
 import jax
 import jax.numpy as jnp
 from jax import lax
+from jax.experimental import pallas as pl
+from jax.experimental.pallas import tpu as pltpu
 from jax.sharding import PartitionSpec as P
+
+MESH = pl.DeviceIdType.MESH
+F32 = jnp.float32
+BF16 = jnp.bfloat16
+I32 = jnp.int32
+
+N = 32
+DP = 4
+HOME = 1024
+D = 1024
+FS = 32
+LISTS = 2048
+BOOKS, CODES, SUB = 16, 256, 64
+CAP = 42
+OVER = 64
+BLOCKS = 11
+PARTS = ((0, 6), (6, 11))
+FIRST = N * OVER
+SLOTS = FIRST + 128 * BLOCKS
+NEAR = 384
+NOBODY = 32 << 8
+
+
+def dot(a, b):
+    return jnp.dot(a, b, preferred_element_type=F32)
+
+
+def iota(shape, dim):
+    return lax.broadcasted_iota(I32, shape, dim)
+
+
+def onehots(mask):
+    return mask.astype(F32).astype(BF16)
+
+
+def routes(assign_ref, slots_ref):
+    assigned = assign_ref[...]
+    table = slots_ref[...].astype(F32).T.astype(I32)
+    table = jnp.concatenate([table >> 8, table & 255], axis=0).astype(F32).astype(BF16)
+    picked = dot(table, onehots(iota((512, HOME), 0) == (assigned >> 7)))
+    low = iota((128, HOME), 0) == (assigned & 127)
+    upper = jnp.sum(jnp.where(low, picked[:128], 0.0), axis=0, keepdims=True)
+    lower = jnp.sum(jnp.where(low, picked[128:], 0.0), axis=0, keepdims=True)
+    slot = upper.astype(I32) * 256 + lower.astype(I32)
+    target, local = slot >> 11, slot & (LISTS - 1)
+    mine = iota((N, HOME), 0) == target
+    before = onehots(iota((HOME, HOME), 0) < iota((HOME, HOME), 1))
+    ahead = dot(onehots(mine), before)
+    rank = jnp.sum(jnp.where(mine, ahead, 0.0), axis=0, keepdims=True).astype(I32)
+    over = rank >= CAP
+    over_rank = dot(jnp.broadcast_to(onehots(over), (8, HOME)), before)[:1].astype(I32)
+    segment = (target >= 11).astype(I32) + (target >= 22).astype(I32)
+    row = jnp.where(over, 11, target - 11 * segment)
+    lane = jnp.where(over, over_rank, CAP * segment + rank)
+    mine = iota((16, HOME), 0) == row
+    place = onehots(iota((128, HOME), 0) == lane)
+    vector = iota((1, HOME), 1)
+    fields = [vector & 255, vector >> 8, local & 255, local >> 8, jnp.ones_like(vector)]
+    planes = [jnp.where(mine, field.astype(F32), 0.0) for field in fields]
+    planes = jnp.concatenate(planes, axis=0).astype(BF16)
+    held = lax.dot_general(planes, place, (((1,), (1,)), ((), ())), preferred_element_type=F32).astype(I32)
+    index, group, local_low, local_high, valid = (held[16 * j : 16 * (j + 1)] for j in range(5))
+    entry = index + (group << 8) + (local_low << 14) + (local_high << 22)
+    entry = jnp.where(valid > 0, entry, NOBODY)
+    return target * 128 + jnp.where(over, 64 + over_rank, rank), entry
+
+
+def kernel(
+    emb_ref, assign_ref, slots_ref, cent_ref, rot_ref, book_ref, out_ref, flag_ref,
+    xb, send, recv, wide, near, cent, cent_t, rot, rot_t, codes, tab_own, tab_all, tab, tab_over, local_ref,
+    resid, sub, errs, code_ref, ret_send, ret_recv, flag_own, flag_all,
+    x_sem, c_sem, r_sem, own_sem, tab_ss, tab_rs, vec_ss, vec_rs, ret_ss, ret_rs, ag_ss, ag_rs, flag_ss, flag_rs,
+):
+    me = lax.axis_index("lists")
+    replica = lax.axis_index("dp")
+    core = lax.rem(me, 2)
+    x = lax.rem(lax.div(me, 2), 4)
+    z = lax.div(me, 8)
+
+    def peer(k):
+        return lax.rem(me + k, N)
+
+    def back(k):
+        return lax.rem(me + N - k, N)
+
+    barrier = pltpu.get_barrier_semaphore()
+
+    @pl.loop(1, N)
+    def _(k):
+        pl.semaphore_signal(barrier, inc=1, device_id={"lists": peer(k)}, device_id_type=MESH)
+
+    for j in range(1, DP):
+        other = lax.rem(replica + j, DP)
+        pl.semaphore_signal(barrier, inc=1, device_id={"dp": other}, device_id_type=MESH)
+
+    def x_copy(t):
+        block = lax.div(t, 12)
+        group = t - block * 12
+        return pltpu.make_async_copy(
+            emb_ref.at[:, pl.ds(pl.multiple_of(t * 256, 256), 256)],
+            xb.at[block, pl.ds(pl.multiple_of(group * FS, FS), FS), :],
+            x_sem.at[t],
+        )
+
+    @pl.loop(0, 128)
+    def _(t):
+        x_copy(t).start()
+
+    c_copy = pltpu.make_async_copy(cent_ref, cent, c_sem)
+    r_copy = pltpu.make_async_copy(rot_ref, rot, r_sem)
+    c_copy.start()
+    r_copy.start()
+
+    code, entry = routes(assign_ref, slots_ref)
+    code_ref[...] = code
+    tab_own[...] = entry
+
+    pl.semaphore_wait(barrier, N - 1 + DP - 1)
+
+    def tab_copy(k, home):
+        return pltpu.make_async_remote_copy(
+            src_ref=tab_own,
+            dst_ref=tab_all.at[home],
+            send_sem=tab_ss.at[k],
+            recv_sem=tab_rs.at[k],
+            device_id={"lists": peer(k)},
+            device_id_type=MESH,
+        )
+
+    @pl.loop(1, N)
+    def _(k):
+        tab_copy(k, me).start()
+
+    tab_all[me] = entry
+    tab_all[N] = jnp.full((16, 128), NOBODY, I32)
+    xb[BLOCKS - 1, 256:, :] = jnp.zeros((128, 256), BF16)
+    sub[:, SUB:, :] = jnp.ones((8, SUB, 1024), BF16)
+
+    @pl.loop(0, BOOKS)
+    def _(m):
+        words = book_ref[m].astype(F32)
+        norm = jnp.sum(words * words, axis=0, keepdims=True)
+        first = norm.astype(BF16).astype(F32)
+        second = (norm - first).astype(BF16).astype(F32)
+        third = norm - first - second
+        row = iota((SUB, CODES), 0)
+        extra = jnp.where(row == 0, first, jnp.where(row == 1, second, jnp.where(row == 2, third, 0.0)))
+        codes[m] = jnp.concatenate([words * -2.0, extra], axis=0).T.astype(BF16)
+
+    r_copy.wait()
+    c_copy.wait()
+
+    @pl.loop(0, 4)
+    def _(i):
+        rows = pl.multiple_of(i * 256, 256)
+        for j in range(4):
+            rot_t[256 * j : 256 * (j + 1), pl.ds(rows, 256)] = rot[pl.ds(rows, 256), 256 * j : 256 * (j + 1)].T
+
+    @pl.loop(0, 8)
+    def _(i):
+        rows = pl.multiple_of(i * 256, 256)
+        for j in range(4):
+            cent_t[256 * j : 256 * (j + 1), pl.ds(rows, 256)] = cent[pl.ds(rows, 256), 256 * j : 256 * (j + 1)].T
+
+    @pl.loop(0, 128)
+    def _(t):
+        x_copy(t).wait()
+
+    @pl.loop(1, N)
+    def _(k):
+        tab_copy(k, back(k)).wait_recv()
+
+    lane = iota((16, 128), 1)
+
+    @pl.loop(0, BLOCKS)
+    def _(b):
+        homes = [tab_all[3 * b + j] + (j << 10) for j in range(3)]
+        for s in range(3):
+            moved = [pltpu.roll(homes[j], (CAP * (j - s)) % 128, 1) if j != s else homes[j] for j in range(3)]
+            found = jnp.where(lane < CAP, moved[0], jnp.where(lane < 2 * CAP, moved[1], moved[2]))
+            tab[b, s] = jnp.where(lane < 3 * CAP, found, NOBODY)
+
+    late = jnp.zeros((1, 128), I32)
+    first_half = iota((1, 128), 1) < OVER
+    for p in range(N // 2):
+        left, right = tab_all[2 * p, 11:12, :], tab_all[2 * p + 1, 11:12, :]
+        tab_over[p : p + 1, :] = jnp.where(first_half, left, pltpu.roll(right, OVER, 1) + (4 << 8))
+        for row in (left, right):
+            late = jnp.where(first_half | (((row >> 8) & 63) >= 32), late, 1)
+        local_ref[:, 128 * p : 128 * (p + 1)] = tab_over[p : p + 1, :] >> 14
+    late = jnp.max(late, axis=1, keepdims=True)
+    flag_own[...] = jnp.broadcast_to(late, (8, 128))
+
+    def flag_copy(j, origin):
+        return pltpu.make_async_remote_copy(
+            src_ref=flag_own,
+            dst_ref=flag_all.at[origin],
+            send_sem=flag_ss.at[j],
+            recv_sem=flag_rs.at[j],
+            device_id={"dp": lax.rem(replica + j, DP)},
+            device_id_type=MESH,
+        )
+
+    for j in range(1, DP):
+        flag_copy(j, replica).start()
+
+    def at_owner(b, owner):
+        segment = lax.div(owner, 11)
+        return tab[b, segment, pl.ds(owner - 11 * segment, 1), :]
+
+    for b in range(BLOCKS):
+        local_ref[:, FIRST + 128 * b : FIRST + 128 * (b + 1)] = at_owner(b, me) >> 14
+
+    mine = pl.ds(pl.multiple_of(core * FS, FS), FS)
+    for p in range(N // 2):
+        entries = tab_over[p : p + 1, :]
+        onehot = onehots(iota((256, 128), 0) == (entries & 255))
+        groups = jnp.broadcast_to((entries >> 8) & 63, (FS, 128))
+        kept = jnp.zeros((FS, 128), F32)
+        for j in range(2):
+            home = 2 * p + j
+            every = dot(xb[home // 3, 128 * (home % 3) : 128 * (home % 3 + 1), :], onehot)
+            for g in range(4):
+                kept = jnp.where(groups == 4 * j + g, every[FS * g : FS * (g + 1)], kept)
+        wide[p // 8, z, x, mine, 128 * (p % 8) : 128 * (p % 8 + 1)] = kept.astype(BF16)
+
+    def along_x(j):
+        return (z * 4 + lax.rem(x + j, 4)) * 2 + core
+
+    def along_z(j):
+        return (lax.rem(z + j, 4) * 4 + x) * 2 + core
+
+    def ag_copy(slot, part, device):
+        return pltpu.make_async_remote_copy(
+            src_ref=part,
+            dst_ref=part,
+            send_sem=ag_ss.at[slot],
+            recv_sem=ag_rs.at[slot],
+            device_id={"lists": device},
+            device_id_type=MESH,
+        )
+
+    def phase(number):
+        copies = []
+        for half in range(2):
+            near_one, far_one = (along_x, along_z) if half == 0 else (along_z, along_x)
+            for j in range(1, 4):
+                slot = 6 * (number - 1) + 3 * half + j - 1
+                if number == 1:
+                    copies.append((slot, wide.at[half, z, x, mine, :], near_one(j)))
+                elif number == 2 and half == 0:
+                    copies.append((slot, wide.at[half, z, :, mine, :], far_one(j)))
+                elif number == 2:
+                    copies.append((slot, wide.at[half, :, x, mine, :], far_one(j)))
+            if number == 3:
+                copies.append((12 + half, wide.at[half, :, :, mine, :], me + 1 - 2 * core))
+        return copies
+
+    def start_phase(number):
+        for copy in phase(number):
+            ag_copy(*copy).start()
+
+    def wait_phase(number):
+        before = lambda v, j: lax.rem(v + 4 - j, 4)
+        theirs = pl.ds(pl.multiple_of((1 - core) * FS, FS), FS)
+        for half in range(2):
+            for j in range(1, 4):
+                slot = 6 * (number - 1) + 3 * half + j - 1
+                if number == 1:
+                    part = wide.at[half, z, before(x, j), mine, :] if half == 0 else wide.at[half, before(z, j), x, mine, :]
+                elif number == 2:
+                    part = wide.at[half, before(z, j), :, mine, :] if half == 0 else wide.at[half, :, before(x, j), mine, :]
+                else:
+                    slot, part = 12 + half, wide.at[half, :, :, theirs, :]
+                if number < 3 or j == 1:
+                    ag_copy(slot, part, peer(1)).wait_recv()
+
+    start_phase(1)
+
+    def vec_copy(part, k, slice_of):
+        low, high = PARTS[part]
+        return pltpu.make_async_remote_copy(
+            src_ref=send.at[k, low:high],
+            dst_ref=recv.at[low:high, pl.ds(pl.multiple_of(slice_of * FS, FS), FS), :],
+            send_sem=vec_ss.at[part, k],
+            recv_sem=vec_rs.at[part, k],
+            device_id={"lists": peer(k)},
+            device_id_type=MESH,
+        )
+
+    def own_copy(part):
+        low, high = PARTS[part]
+        return pltpu.make_async_copy(
+            send.at[0, low:high],
+            recv.at[low:high, pl.ds(pl.multiple_of(me * FS, FS), FS), :],
+            own_sem.at[part],
+        )
+
+    def select_part(part):
+        @pl.loop(0, N // 2)
+        def _(i):
+            owners = [peer(2 * i), peer(2 * i + 1)]
+            for b in range(*PARTS[part]):
+                entries = jnp.concatenate([at_owner(b, owner) for owner in owners], axis=1)
+                every = dot(xb[b], onehots(iota((256, 256), 0) == (entries & 255)))
+                groups = jnp.broadcast_to((entries >> 8) & 63, (FS, 256))
+                kept = jnp.zeros((FS, 256), F32)
+                for g in range(12):
+                    kept = jnp.where(groups == g, every[FS * g : FS * (g + 1)], kept)
+                kept = kept.astype(BF16)
+                send[2 * i, b] = kept[:, :128]
+                send[2 * i + 1, b] = kept[:, 128:]
+
+            @pl.when(i == 0)
+            def _():
+                own_copy(part).start()
+
+            @pl.when(i > 0)
+            def _():
+                vec_copy(part, 2 * i, me).start()
+
+            vec_copy(part, 2 * i + 1, me).start()
+
+    select_part(0)
+    wait_phase(1)
+    start_phase(2)
+    select_part(1)
+
+    @pl.loop(0, SLOTS // NEAR)
+    def _(t):
+        lanes = pl.ds(pl.multiple_of(t * NEAR, 128), NEAR)
+        onehot = onehots(iota((LISTS, NEAR), 0) == local_ref[:, lanes])
+        near[:, lanes] = dot(cent_t[...], onehot).astype(BF16)
+
+        @pl.when(t == 5)
+        def _():
+            wait_phase(2)
+            start_phase(3)
+
+    def encode(width, lanes):
+        @pl.loop(0, 2)
+        def _(i):
+            rows = pl.ds(pl.multiple_of(i * 512, 512), 512)
+            turned = dot(rot_t[rows, :], resid[:, :width]).astype(BF16)
+            for j in range(8):
+                piece = turned[SUB * j : SUB * (j + 1)]
+                sub[j, :SUB, :width] = piece
+                squares = piece.astype(F32)
+                length = jnp.sum(squares * squares, axis=0, keepdims=True)
+                least = jnp.min(dot(codes[8 * i + j], sub[j, :, :width]), axis=0, keepdims=True)
+                errs[pl.ds(8 * i + j, 1), lanes] = (length + least) * (1.0 / SUB)
+
+    def minus(a, b):
+        return (a.astype(F32) - b.astype(F32)).astype(BF16)
+
+    wait_phase(3)
+
+    @pl.loop(0, 2)
+    def _(half):
+        lanes = pl.ds(pl.multiple_of(half * 1024, 1024), 1024)
+
+        @pl.loop(0, 4)
+        def _(i):
+            for j in range(4):
+                rows = pl.ds(pl.multiple_of(i * 256 + j * 64, 64), 64)
+                resid[rows, :] = minus(wide[half, i, j], near[rows, lanes])
+
+        encode(1024, lanes)
+
+    def ret_copy(home, owner):
+        return pltpu.make_async_remote_copy(
+            src_ref=ret_send.at[home],
+            dst_ref=ret_recv.at[owner],
+            send_sem=ret_ss.at[home],
+            recv_sem=ret_rs.at[owner],
+            device_id={"lists": home},
+            device_id_type=MESH,
+        )
+
+    main_lanes = iota((BOOKS, 128), 1) < 64
+    for part, (low, high) in enumerate(PARTS):
+        own_copy(part).wait()
+
+        @pl.loop(1, N)
+        def _(k):
+            vec_copy(part, k, back(k)).wait_recv()
+
+        width, base = 128 * (high - low), FIRST + 128 * low
+
+        @pl.loop(0, 4)
+        def _(i):
+            rows = pl.ds(pl.multiple_of(i * 256, 256), 256)
+            for b in range(low, high):
+                resid[rows, 128 * (b - low) : 128 * (b - low + 1)] = minus(
+                    recv[b, rows, :], near[rows, FIRST + 128 * b : FIRST + 128 * (b + 1)]
+                )
+
+        encode(width, slice(base, base + width))
+
+        for home in range(3 * low, min(3 * high, N)):
+            main = errs[:, FIRST + 128 * (home // 3) : FIRST + 128 * (home // 3 + 1)]
+            if home % 3:
+                main = pltpu.roll(main, 128 - CAP * (home % 3), 1)
+            more = errs[:, 128 * (home // 2) : 128 * (home // 2 + 1)]
+            if home % 2 == 0:
+                more = pltpu.roll(more, OVER, 1)
+            ret_send[home] = jnp.where(main_lanes, main, more)
+
+        @pl.loop(3 * low, min(3 * high, N))
+        def _(home):
+            @pl.when(home == me)
+            def _():
+                ret_recv[home] = ret_send[home]
+
+            @pl.when(home != me)
+            def _():
+                ret_copy(home, me).start()
+
+    for j in range(1, DP):
+        flag_copy(j, lax.rem(replica + DP - j, DP)).wait_recv()
+        late = jnp.maximum(late, flag_all[lax.rem(replica + DP - j, DP)][:1, :1])
+    flag_ref[...] = jnp.broadcast_to(late, (8, 128))
+
+    @pl.loop(1, N)
+    def _(k):
+        ret_copy(me, peer(k)).wait_recv()
+
+    total = jnp.zeros((2 * BOOKS, HOME), F32)
+    for t in range(N // 2):
+        got = jnp.concatenate([ret_recv[2 * t], ret_recv[2 * t + 1]], axis=1)
+        high = got.astype(BF16)
+        low = (got - high.astype(F32)).astype(BF16)
+        onehot = onehots(iota((256, HOME), 0) + 256 * t == code_ref[...])
+        total = total + dot(jnp.concatenate([high, low], axis=0), onehot)
+    out_ref[...] = total[:BOOKS] + total[BOOKS:]
+
+    @pl.loop(1, N)
+    def _(k):
+        tab_copy(k, me).wait_send()
+        ret_copy(peer(k), me).wait_send()
+        for part in range(len(PARTS)):
+            vec_copy(part, k, me).wait_send()
+
+    for number in range(1, 4):
+        for copy in phase(number):
+            ag_copy(*copy).wait_send()
+    for j in range(1, DP):
+        flag_copy(j, replica).wait_send()
+
+
+def fast(embeddings, assign, list_slot, centroids, rotation, codebook):
+    vmem = pl.BlockSpec(memory_space=pltpu.VMEM)
+    hbm = pl.BlockSpec(memory_space=pl.ANY)
+    dma = pltpu.SemaphoreType.DMA
+    return pl.pallas_call(
+        kernel,
+        out_shape=(jax.ShapeDtypeStruct((BOOKS, HOME), F32), jax.ShapeDtypeStruct((8, 128), I32)),
+        in_specs=[hbm, vmem, vmem, hbm, hbm, vmem],
+        out_specs=(vmem, vmem),
+        scratch_shapes=[
+            pltpu.VMEM((BLOCKS, 384, 256), BF16),
+            pltpu.VMEM((N, BLOCKS, FS, 128), BF16),
+            pltpu.VMEM((BLOCKS, D, 128), BF16),
+            pltpu.VMEM((2, 4, 4, 2 * FS, 1024), BF16),
+            pltpu.VMEM((D, SLOTS), BF16),
+            pltpu.VMEM((LISTS, D), BF16),
+            pltpu.VMEM((D, LISTS), BF16),
+            pltpu.VMEM((D, D), BF16),
+            pltpu.VMEM((D, D), BF16),
+            pltpu.VMEM((BOOKS, CODES, 2 * SUB), BF16),
+            pltpu.VMEM((16, 128), I32),
+            pltpu.VMEM((N + 1, 16, 128), I32),
+            pltpu.VMEM((BLOCKS, 3, 16, 128), I32),
+            pltpu.VMEM((N // 2, 128), I32),
+            pltpu.VMEM((1, SLOTS), I32),
+            pltpu.VMEM((D, 1024), BF16),
+            pltpu.VMEM((8, 2 * SUB, 1024), BF16),
+            pltpu.VMEM((BOOKS, SLOTS), F32),
+            pltpu.VMEM((1, HOME), I32),
+            pltpu.VMEM((N, BOOKS, 128), F32),
+            pltpu.VMEM((N, BOOKS, 128), F32),
+            pltpu.VMEM((8, 128), I32),
+            pltpu.VMEM((DP, 8, 128), I32),
+            dma((128,)), dma, dma, dma((len(PARTS),)),
+            dma((N,)), dma((N,)),
+            dma((len(PARTS), N)), dma((len(PARTS), N)),
+            dma((N,)), dma((N,)),
+            dma((14,)), dma((14,)),
+            dma((DP,)), dma((DP,)),
+        ],
+        compiler_params=pltpu.CompilerParams(
+            collective_id=0, has_side_effects=True, vmem_limit_bytes=58 * 2**20
+        ),
+        name="encode",
+    )(
+        embeddings.T,
+        assign.reshape(1, HOME),
+        list_slot.reshape(512, 128),
+        centroids,
+        rotation.reshape(D, D),
+        codebook.transpose(0, 2, 1),
+    )
 
 
 def route_rows(assigned, list_slot, list_width, owner_count):
@@ -41,7 +545,7 @@
     return lax.all_to_all(errors, "lists", split_axis=0, concat_axis=0, tiled=True)
 
 
-def shards(embeddings, assign, list_slot, centroids, rotation, codebook):
+def general(embeddings, assign, list_slot, centroids, rotation, codebook):
     owner_count = lax.axis_size("lists")
     list_width = centroids.shape[0]
     home_rows = assign.shape[0]
@@ -67,6 +571,11 @@
     return jnp.transpose(returned, (1, 0, 2))[:, target, position]
 
 
+def shards(*arrays):
+    errors, flag = fast(*arrays)
+    return lax.cond(flag[0, 0] > 0, lambda: general(*arrays), lambda: errors)
+
+
 def solution(mesh):
     placed = (
         P("dp", "lists"),

time: 301 us -> 94.5 us (0.31)
  the two profiles are of different devices: /device:TPU:1 before, /device:TPU:97 now
where the time goes in v2:
time: 94.5 us; the launch traced here: 94.1 us
  Pallas kernels  91.5 us (97%)
  local copies, waits for them, and re-layouts  1.84 us (2%)
    pallas_call x1, Pallas kernels, fast(): pl.pallas_call(kernel, out_shape=(jax.ShapeDtypeStruct((BOOKS, HOME), F32...  91.5 us

profile of v2, /device:TPU:97, one launch (start us, length us, event | category | flops | bytes accessed | tf_op | source)
XLA Modules:
  0.0 94.1 jit_solution(8810408245672299721)
XLA Ops:
  0.0 0.0 copy-start.1
  0.0 0.0 copy-start.4
  0.0 0.0 copy-start
  0.0 0.0 copy-start.2
  0.0 91.5 %encode.1 = (f32[16,1024]{1,0:T(8,128)S(1)}, s32[8,128]{1,0:T(8,128)}) custom-call(bf16[32,32768]{1,0:T(8,128)(2,1)} %bitcast.64, s32[1,1024]{1,0:T(1,128)} %bitcast.80, s32[512,128]{1,0:T(8,128)} %bitcast.58, bf16[2048,1024]{1,0:T(8,128)(2,1)} %cent_ref.1, bf16[1024,1024]{1,0:T(8,128)(2,1)} %bitcast.69, bf16[16,64,256]{2,1,0:T(8,128)(2,1)} %bitcast.68), custom_call_target="tpu_custom_call" | custom-call | tf_op jit(solution)/shard_map/encode/pallas_call | solution.py:461
  91.6 1.2 %slice.9 = s32[1,1]{1,0:T(1,128)} slice(s32[8,128]{1,0:T(8,128)} %get-tuple-element.61), slice={[0:1], [0:1]} | slice | bytes 8 | tf_op jit(solution)/shard_map/slice | solution.py:576
  93.4 0.0 copy-done.1
  93.4 0.0 copy-done.4
  93.4 0.0 copy-done
  93.5 0.0 copy-done.2
  93.5 0.6 copy.63
  (1 shorter events, 0.0 us)
Async XLA Ops:
  0.0 93.4 %copy-start.1 = (bf16[32768,32]{0,1:T(8,128)(2,1)S(1)}, bf16[32768,32]{0,1:T(8,128)(2,1)}, u32[]{:S(2)}) copy-start(bf16[32768,32]{0,1:T(8,128)(2,1)} %param.10) | copy-start | bytes 6291460
  0.0 93.4 %copy-start.4 = (s32[1024]{0:T(1024)S(1)}, s32[1024]{0:T(1024)}, u32[]{:S(2)}) copy-start(s32[1024]{0:T(1024)} %param.11) | copy-start | bytes 12292
  0.0 93.4 %copy-start = (s32[65536]{0:T(1024)S(1)}, s32[65536]{0:T(1024)}, u32[]{:S(2)}) copy-start(s32[65536]{0:T(1024)} %param.12) | copy-start | bytes 786436
  0.0 93.4 %copy-start.2 = (bf16[16,256,64]{1,2,0:T(8,128)(2,1)S(1)}, bf16[16,256,64]{1,2,0:T(8,128)(2,1)}, u32[]{:S(2)}) copy-start(bf16[16,256,64]{1,2,0:T(8,128)(2,1)} %param.15) | copy-start | bytes 1572868

commit v3 on v2

--- a/solution.py
+++ b/solution.py
@@ -23,7 +23,9 @@
 PARTS = ((0, 6), (6, 11))
 FIRST = N * OVER
 SLOTS = FIRST + 128 * BLOCKS
-NEAR = 384
+NEAR = 512
+PHASE = 6
+NEARS = -(-SLOTS // NEAR)
 NOBODY = 32 << 8
 
 
@@ -214,6 +216,7 @@
         segment = lax.div(owner, 11)
         return tab[b, segment, pl.ds(owner - 11 * segment, 1), :]
 
+    local_ref[:, SLOTS:] = jnp.zeros((1, NEARS * NEAR - SLOTS), I32)
     for b in range(BLOCKS):
         local_ref[:, FIRST + 128 * b : FIRST + 128 * (b + 1)] = at_owner(b, me) >> 14
 
@@ -283,14 +286,18 @@
 
     start_phase(1)
 
-    def vec_copy(part, k, slice_of):
+    def across(i):
+        chip = lax.rem(z + lax.rem(i, 4), 4) * 4 + lax.rem(x + lax.rem(lax.div(i, 4) + i, 4), 4)
+        return [chip * 2 + core, chip * 2 + 1 - core]
+
+    def vec_copy(part, k, owner, slice_of):
         low, high = PARTS[part]
         return pltpu.make_async_remote_copy(
             src_ref=send.at[k, low:high],
             dst_ref=recv.at[low:high, pl.ds(pl.multiple_of(slice_of * FS, FS), FS), :],
             send_sem=vec_ss.at[part, k],
-            recv_sem=vec_rs.at[part, k],
-            device_id={"lists": peer(k)},
+            recv_sem=vec_rs.at[part, slice_of],
+            device_id={"lists": owner},
             device_id_type=MESH,
         )
 
@@ -305,7 +312,7 @@
     def select_part(part):
         @pl.loop(0, N // 2)
         def _(i):
-            owners = [peer(2 * i), peer(2 * i + 1)]
+            owners = across(i)
             for b in range(*PARTS[part]):
                 entries = jnp.concatenate([at_owner(b, owner) for owner in owners], axis=1)
                 every = dot(xb[b], onehots(iota((256, 256), 0) == (entries & 255)))
@@ -323,22 +330,22 @@
 
             @pl.when(i > 0)
             def _():
-                vec_copy(part, 2 * i, me).start()
-
-            vec_copy(part, 2 * i + 1, me).start()
+                vec_copy(part, 2 * i, owners[0], me).start()
+
+            vec_copy(part, 2 * i + 1, owners[1], me).start()
 
     select_part(0)
     wait_phase(1)
     start_phase(2)
     select_part(1)
 
-    @pl.loop(0, SLOTS // NEAR)
+    @pl.loop(0, NEARS)
     def _(t):
         lanes = pl.ds(pl.multiple_of(t * NEAR, 128), NEAR)
         onehot = onehots(iota((LISTS, NEAR), 0) == local_ref[:, lanes])
         near[:, lanes] = dot(cent_t[...], onehot).astype(BF16)
 
-        @pl.when(t == 5)
+        @pl.when(t == PHASE)
         def _():
             wait_phase(2)
             start_phase(3)
@@ -359,20 +366,6 @@
     def minus(a, b):
         return (a.astype(F32) - b.astype(F32)).astype(BF16)
 
-    wait_phase(3)
-
-    @pl.loop(0, 2)
-    def _(half):
-        lanes = pl.ds(pl.multiple_of(half * 1024, 1024), 1024)
-
-        @pl.loop(0, 4)
-        def _(i):
-            for j in range(4):
-                rows = pl.ds(pl.multiple_of(i * 256 + j * 64, 64), 64)
-                resid[rows, :] = minus(wide[half, i, j], near[rows, lanes])
-
-        encode(1024, lanes)
-
     def ret_copy(home, owner):
         return pltpu.make_async_remote_copy(
             src_ref=ret_send.at[home],
@@ -383,13 +376,29 @@
             device_id_type=MESH,
         )
 
+    def overflow():
+        wait_phase(3)
+
+        @pl.loop(0, 2)
+        def _(half):
+            lanes = pl.ds(pl.multiple_of(half * 1024, 1024), 1024)
+
+            @pl.loop(0, 4)
+            def _(i):
+                for j in range(4):
+                    rows = pl.ds(pl.multiple_of(i * 256 + j * 64, 64), 64)
+                    resid[rows, :] = minus(wide[half, i, j], near[rows, lanes])
+
+            encode(1024, lanes)
+
     main_lanes = iota((BOOKS, 128), 1) < 64
-    for part, (low, high) in enumerate(PARTS):
+    def main(part):
+        low, high = PARTS[part]
         own_copy(part).wait()
 
         @pl.loop(1, N)
         def _(k):
-            vec_copy(part, k, back(k)).wait_recv()
+            vec_copy(part, k, peer(1), back(k)).wait_recv()
 
         width, base = 128 * (high - low), FIRST + 128 * low
 
@@ -403,14 +412,16 @@
 
         encode(width, slice(base, base + width))
 
+    def give_back(part):
+        low, high = PARTS[part]
         for home in range(3 * low, min(3 * high, N)):
-            main = errs[:, FIRST + 128 * (home // 3) : FIRST + 128 * (home // 3 + 1)]
+            least = errs[:, FIRST + 128 * (home // 3) : FIRST + 128 * (home // 3 + 1)]
             if home % 3:
-                main = pltpu.roll(main, 128 - CAP * (home % 3), 1)
+                least = pltpu.roll(least, 128 - CAP * (home % 3), 1)
             more = errs[:, 128 * (home // 2) : 128 * (home // 2 + 1)]
             if home % 2 == 0:
                 more = pltpu.roll(more, OVER, 1)
-            ret_send[home] = jnp.where(main_lanes, main, more)
+            ret_send[home] = jnp.where(main_lanes, least, more)
 
         @pl.loop(3 * low, min(3 * high, N))
         def _(home):
@@ -421,6 +432,12 @@
             @pl.when(home != me)
             def _():
                 ret_copy(home, me).start()
+
+    main(0)
+    overflow()
+    give_back(0)
+    main(1)
+    give_back(1)
 
     for j in range(1, DP):
         flag_copy(j, lax.rem(replica + DP - j, DP)).wait_recv()
@@ -445,7 +462,7 @@
         tab_copy(k, me).wait_send()
         ret_copy(peer(k), me).wait_send()
         for part in range(len(PARTS)):
-            vec_copy(part, k, me).wait_send()
+            vec_copy(part, k, peer(1), me).wait_send()
 
     for number in range(1, 4):
         for copy in phase(number):
@@ -468,7 +485,7 @@
             pltpu.VMEM((N, BLOCKS, FS, 128), BF16),
             pltpu.VMEM((BLOCKS, D, 128), BF16),
             pltpu.VMEM((2, 4, 4, 2 * FS, 1024), BF16),
-            pltpu.VMEM((D, SLOTS), BF16),
+            pltpu.VMEM((D, NEARS * NEAR), BF16),
             pltpu.VMEM((LISTS, D), BF16),
             pltpu.VMEM((D, LISTS), BF16),
             pltpu.VMEM((D, D), BF16),
@@ -478,7 +495,7 @@
             pltpu.VMEM((N + 1, 16, 128), I32),
             pltpu.VMEM((BLOCKS, 3, 16, 128), I32),
             pltpu.VMEM((N // 2, 128), I32),
-            pltpu.VMEM((1, SLOTS), I32),
+            pltpu.VMEM((1, NEARS * NEAR), I32),
             pltpu.VMEM((D, 1024), BF16),
             pltpu.VMEM((8, 2 * SUB, 1024), BF16),
             pltpu.VMEM((BOOKS, SLOTS), F32),

time: 94.5 us -> 89.7 us (0.949)
  Pallas kernels: 91.5 us -> 87 us
    pallas_call x1, Pallas kernels: 91.5 us -> 87 us  [fast(): pl.pallas_call(kernel, out_shape=(jax.ShapeDtypeStruct((BOOKS, HOME), F32...]
where the time goes in v3:
time: 89.7 us; the launch traced here: 89.5 us
  Pallas kernels  87 us (97%)
  local copies, waits for them, and re-layouts  1.84 us (2%)
    pallas_call x1, Pallas kernels, fast(): pl.pallas_call(kernel, out_shape=(jax.ShapeDtypeStruct((BOOKS, HOME), F32...  87 us

profile of v3, /device:TPU:97, one launch (start us, length us, event | category | flops | bytes accessed | tf_op | source)
XLA Modules:
  0.0 89.5 jit_solution(17207777096218086060)
XLA Ops:
  0.0 0.0 copy-start.1
  0.0 0.0 copy-start.4
  0.0 0.0 copy-start
  0.0 0.0 copy-start.2
  0.0 87.0 %encode.1 = (f32[16,1024]{1,0:T(8,128)S(1)}, s32[8,128]{1,0:T(8,128)}) custom-call(bf16[32,32768]{1,0:T(8,128)(2,1)} %bitcast.64, s32[1,1024]{1,0:T(1,128)} %bitcast.80, s32[512,128]{1,0:T(8,128)} %bitcast.58, bf16[2048,1024]{1,0:T(8,128)(2,1)} %cent_ref.1, bf16[1024,1024]{1,0:T(8,128)(2,1)} %bitcast.69, bf16[16,64,256]{2,1,0:T(8,128)(2,1)} %bitcast.68), custom_call_target="tpu_custom_call" | custom-call | tf_op jit(solution)/shard_map/encode/pallas_call | solution.py:478
  87.0 1.2 %slice.9 = s32[1,1]{1,0:T(1,128)} slice(s32[8,128]{1,0:T(8,128)} %get-tuple-element.61), slice={[0:1], [0:1]} | slice | bytes 8 | tf_op jit(solution)/shard_map/slice | solution.py:593
  88.9 0.0 copy-done.1
  88.9 0.0 copy-done.4
  88.9 0.0 copy-done
  88.9 0.0 copy-done.2
  88.9 0.6 copy.63
  (1 shorter events, 0.0 us)
Async XLA Ops:
  0.0 88.9 %copy-start.1 = (bf16[32768,32]{0,1:T(8,128)(2,1)S(1)}, bf16[32768,32]{0,1:T(8,128)(2,1)}, u32[]{:S(2)}) copy-start(bf16[32768,32]{0,1:T(8,128)(2,1)} %param.10) | copy-start | bytes 6291460
  0.0 88.9 %copy-start.4 = (s32[1024]{0:T(1024)S(1)}, s32[1024]{0:T(1024)}, u32[]{:S(2)}) copy-start(s32[1024]{0:T(1024)} %param.11) | copy-start | bytes 12292
  0.0 88.9 %copy-start = (s32[65536]{0:T(1024)S(1)}, s32[65536]{0:T(1024)}, u32[]{:S(2)}) copy-start(s32[65536]{0:T(1024)} %param.12) | copy-start | bytes 786436
  0.0 88.9 %copy-start.2 = (bf16[16,256,64]{1,2,0:T(8,128)(2,1)S(1)}, bf16[16,256,64]{1,2,0:T(8,128)(2,1)}, u32[]{:S(2)}) copy-start(bf16[16,256,64]{1,2,0:T(8,128)(2,1)} %param.15) | copy-start | bytes 1572868

commit v4 on v3

--- a/solution.py
+++ b/solution.py
@@ -20,11 +20,14 @@
 CAP = 42
 OVER = 64
 BLOCKS = 11
-PARTS = ((0, 6), (6, 11))
+PARTS = ((0, 4), (4, 8), (8, 11))
 FIRST = N * OVER
 SLOTS = FIRST + 128 * BLOCKS
 NEAR = 512
-PHASE = 6
+GROUP = 4
+EARLY = 2
+PHASE = 2
+LATER = {1: 1, 2: 3}
 NEARS = -(-SLOTS // NEAR)
 NOBODY = 32 << 8
 
@@ -265,9 +268,17 @@
                 copies.append((12 + half, wide.at[half, :, :, mine, :], me + 1 - 2 * core))
         return copies
 
+    def pieces(number, slot, part):
+        if number == 1:
+            return [part]
+        if number == 2:
+            return [part.at[q, :, 512 * h : 512 * (h + 1)] for q in range(4) for h in range(2)]
+        return [part.at[q, r] for q in range(4) for r in range(4)]
+
     def start_phase(number):
-        for copy in phase(number):
-            ag_copy(*copy).start()
+        for slot, part, device in phase(number):
+            for piece in pieces(number, slot, part):
+                ag_copy(slot, piece, device).start()
 
     def wait_phase(number):
         before = lambda v, j: lax.rem(v + 4 - j, 4)
@@ -309,41 +320,60 @@
             own_sem.at[part],
         )
 
+    def send_to(part, i):
+        owners = across(i)
+
+        @pl.when(i == 0)
+        def _():
+            own_copy(part).start()
+
+        @pl.when(i > 0)
+        def _():
+            vec_copy(part, 2 * i, owners[0], me).start()
+
+        vec_copy(part, 2 * i + 1, owners[1], me).start()
+
     def select_part(part):
-        @pl.loop(0, N // 2)
+        @pl.loop(0, N // GROUP)
         def _(i):
-            owners = across(i)
+            chips = [GROUP // 2 * i + j for j in range(GROUP // 2)]
+            owners = [owner for chip in chips for owner in across(chip)]
             for b in range(*PARTS[part]):
                 entries = jnp.concatenate([at_owner(b, owner) for owner in owners], axis=1)
-                every = dot(xb[b], onehots(iota((256, 256), 0) == (entries & 255)))
-                groups = jnp.broadcast_to((entries >> 8) & 63, (FS, 256))
-                kept = jnp.zeros((FS, 256), F32)
+                every = dot(xb[b], onehots(iota((256, 128 * GROUP), 0) == (entries & 255)))
+                groups = jnp.broadcast_to((entries >> 8) & 63, (FS, 128 * GROUP))
+                kept = jnp.zeros((FS, 128 * GROUP), F32)
                 for g in range(12):
                     kept = jnp.where(groups == g, every[FS * g : FS * (g + 1)], kept)
                 kept = kept.astype(BF16)
-                send[2 * i, b] = kept[:, :128]
-                send[2 * i + 1, b] = kept[:, 128:]
-
-            @pl.when(i == 0)
-            def _():
-                own_copy(part).start()
-
-            @pl.when(i > 0)
-            def _():
-                vec_copy(part, 2 * i, owners[0], me).start()
-
-            vec_copy(part, 2 * i + 1, owners[1], me).start()
-
-    select_part(0)
-    wait_phase(1)
-    start_phase(2)
-    select_part(1)
+                for j in range(GROUP):
+                    send[GROUP * i + j, b] = kept[:, 128 * j : 128 * (j + 1)]
+
+            if part == 0:
+                for chip in chips:
+                    send_to(part, chip)
+
+                @pl.when(i == EARLY)
+                def _():
+                    wait_phase(1)
+                    start_phase(2)
+
+    for part in range(len(PARTS)):
+        select_part(part)
 
     @pl.loop(0, NEARS)
     def _(t):
         lanes = pl.ds(pl.multiple_of(t * NEAR, 128), NEAR)
         onehot = onehots(iota((LISTS, NEAR), 0) == local_ref[:, lanes])
         near[:, lanes] = dot(cent_t[...], onehot).astype(BF16)
+
+        for part, tile in LATER.items():
+
+            @pl.when(t == tile)
+            def _():
+                @pl.loop(0, N // 2)
+                def _(i):
+                    send_to(part, i)
 
         @pl.when(t == PHASE)
         def _():
@@ -433,11 +463,10 @@
             def _():
                 ret_copy(home, me).start()
 
-    main(0)
     overflow()
-    give_back(0)
-    main(1)
-    give_back(1)
+    for part in range(len(PARTS)):
+        main(part)
+        give_back(part)
 
     for j in range(1, DP):
         flag_copy(j, lax.rem(replica + DP - j, DP)).wait_recv()

time: 89.7 us -> 87.4 us (0.974)
  Pallas kernels: 87 us -> 84.7 us
    pallas_call x1, Pallas kernels: 87 us -> 84.7 us  [fast(): pl.pallas_call(kernel, out_shape=(jax.ShapeDtypeStruct((BOOKS, HOME), F32...]
where the time goes in v4:
time: 87.4 us; the launch traced here: 87.2 us
  Pallas kernels  84.7 us (97%)
  local copies, waits for them, and re-layouts  1.84 us (2%)
    pallas_call x1, Pallas kernels, fast(): pl.pallas_call(kernel, out_shape=(jax.ShapeDtypeStruct((BOOKS, HOME), F32...  84.7 us

profile of v4, /device:TPU:97, one launch (start us, length us, event | category | flops | bytes accessed | tf_op | source)
XLA Modules:
  0.0 87.2 jit_solution(9223266056719198907)
XLA Ops:
  0.0 0.0 copy-start.1
  0.0 0.0 copy-start.4
  0.0 0.0 copy-start
  0.0 0.0 copy-start.2
  0.0 84.7 %encode.1 = (f32[16,1024]{1,0:T(8,128)S(1)}, s32[8,128]{1,0:T(8,128)}) custom-call(bf16[32,32768]{1,0:T(8,128)(2,1)} %bitcast.64, s32[1,1024]{1,0:T(1,128)} %bitcast.80, s32[512,128]{1,0:T(8,128)} %bitcast.58, bf16[2048,1024]{1,0:T(8,128)(2,1)} %cent_ref.1, bf16[1024,1024]{1,0:T(8,128)(2,1)} %bitcast.69, bf16[16,64,256]{2,1,0:T(8,128)(2,1)} %bitcast.68), custom_call_target="tpu_custom_call" | custom-call | tf_op jit(solution)/shard_map/encode/pallas_call | solution.py:507
  84.7 1.2 %slice.9 = s32[1,1]{1,0:T(1,128)} slice(s32[8,128]{1,0:T(8,128)} %get-tuple-element.61), slice={[0:1], [0:1]} | slice | bytes 8 | tf_op jit(solution)/shard_map/slice | solution.py:622
  86.5 0.0 copy-done.1
  86.5 0.0 copy-done.4
  86.5 0.0 copy-done
  86.6 0.0 copy-done.2
  86.6 0.6 copy.63
  (1 shorter events, 0.0 us)
Async XLA Ops:
  0.0 86.5 %copy-start.1 = (bf16[32768,32]{0,1:T(8,128)(2,1)S(1)}, bf16[32768,32]{0,1:T(8,128)(2,1)}, u32[]{:S(2)}) copy-start(bf16[32768,32]{0,1:T(8,128)(2,1)} %param.10) | copy-start | bytes 6291460
  0.0 86.5 %copy-start.4 = (s32[1024]{0:T(1024)S(1)}, s32[1024]{0:T(1024)}, u32[]{:S(2)}) copy-start(s32[1024]{0:T(1024)} %param.11) | copy-start | bytes 12292
  0.0 86.5 %copy-start = (s32[65536]{0:T(1024)S(1)}, s32[65536]{0:T(1024)}, u32[]{:S(2)}) copy-start(s32[65536]{0:T(1024)} %param.12) | copy-start | bytes 786436
  0.0 86.5 %copy-start.2 = (bf16[16,256,64]{1,2,0:T(8,128)(2,1)S(1)}, bf16[16,256,64]{1,2,0:T(8,128)(2,1)}, u32[]{:S(2)}) copy-start(bf16[16,256,64]{1,2,0:T(8,128)(2,1)} %param.15) | copy-start | bytes 1572868

commit v5 on v4

--- a/solution.py
+++ b/solution.py
@@ -91,8 +91,21 @@
     def peer(k):
         return lax.rem(me + k, N)
 
-    def back(k):
-        return lax.rem(me + N - k, N)
+    def all_of(ref, send_sem, recv_sem):
+        return pltpu.make_async_remote_copy(
+            src_ref=ref, dst_ref=ref, send_sem=send_sem, recv_sem=recv_sem,
+            device_id={"lists": peer(1)}, device_id_type=MESH,
+        )
+
+    def all_tables():
+        return all_of(tab_all.at[: N - 1], tab_ss, tab_rs)
+
+    def all_vectors(part):
+        low, high = PARTS[part]
+        return all_of(send.at[1:, low:high], vec_ss.at[part], vec_rs.at[part])
+
+    def all_returns():
+        return all_of(ret_recv.at[: N - 1], ret_ss, ret_rs)
 
     barrier = pltpu.get_barrier_semaphore()
 
@@ -110,12 +123,8 @@
         return pltpu.make_async_copy(
             emb_ref.at[:, pl.ds(pl.multiple_of(t * 256, 256), 256)],
             xb.at[block, pl.ds(pl.multiple_of(group * FS, FS), FS), :],
-            x_sem.at[t],
-        )
-
-    @pl.loop(0, 128)
-    def _(t):
-        x_copy(t).start()
+            x_sem.at[lax.div(t, 120)],
+        )
 
     c_copy = pltpu.make_async_copy(cent_ref, cent, c_sem)
     r_copy = pltpu.make_async_copy(rot_ref, rot, r_sem)
@@ -132,8 +141,8 @@
         return pltpu.make_async_remote_copy(
             src_ref=tab_own,
             dst_ref=tab_all.at[home],
-            send_sem=tab_ss.at[k],
-            recv_sem=tab_rs.at[k],
+            send_sem=tab_ss,
+            recv_sem=tab_rs,
             device_id={"lists": peer(k)},
             device_id_type=MESH,
         )
@@ -141,6 +150,10 @@
     @pl.loop(1, N)
     def _(k):
         tab_copy(k, me).start()
+
+    @pl.loop(0, 128)
+    def _(t):
+        x_copy(t).start()
 
     tab_all[me] = entry
     tab_all[N] = jnp.full((16, 128), NOBODY, I32)
@@ -173,13 +186,10 @@
         for j in range(4):
             cent_t[256 * j : 256 * (j + 1), pl.ds(rows, 256)] = cent[pl.ds(rows, 256), 256 * j : 256 * (j + 1)].T
 
-    @pl.loop(0, 128)
-    def _(t):
-        x_copy(t).wait()
-
-    @pl.loop(1, N)
-    def _(k):
-        tab_copy(k, back(k)).wait_recv()
+    pltpu.make_async_copy(xb.at[:10], xb.at[:10], x_sem.at[0]).wait()
+    pltpu.make_async_copy(xb.at[10, :256], xb.at[10, :256], x_sem.at[1]).wait()
+
+    all_tables().wait_recv()
 
     lane = iota((16, 128), 1)
 
@@ -272,8 +282,8 @@
         if number == 1:
             return [part]
         if number == 2:
-            return [part.at[q, :, 512 * h : 512 * (h + 1)] for q in range(4) for h in range(2)]
-        return [part.at[q, r] for q in range(4) for r in range(4)]
+            return [part.at[q] for q in range(4)]
+        return [part.at[q] for q in range(4)]
 
     def start_phase(number):
         for slot, part, device in phase(number):
@@ -306,8 +316,8 @@
         return pltpu.make_async_remote_copy(
             src_ref=send.at[k, low:high],
             dst_ref=recv.at[low:high, pl.ds(pl.multiple_of(slice_of * FS, FS), FS), :],
-            send_sem=vec_ss.at[part, k],
-            recv_sem=vec_rs.at[part, slice_of],
+            send_sem=vec_ss.at[part],
+            recv_sem=vec_rs.at[part],
             device_id={"lists": owner},
             device_id_type=MESH,
         )
@@ -400,8 +410,8 @@
         return pltpu.make_async_remote_copy(
             src_ref=ret_send.at[home],
             dst_ref=ret_recv.at[owner],
-            send_sem=ret_ss.at[home],
-            recv_sem=ret_rs.at[owner],
+            send_sem=ret_ss,
+            recv_sem=ret_rs,
             device_id={"lists": home},
             device_id_type=MESH,
         )
@@ -426,9 +436,7 @@
         low, high = PARTS[part]
         own_copy(part).wait()
 
-        @pl.loop(1, N)
-        def _(k):
-            vec_copy(part, k, peer(1), back(k)).wait_recv()
+        all_vectors(part).wait_recv()
 
         width, base = 128 * (high - low), FIRST + 128 * low
 
@@ -473,9 +481,16 @@
         late = jnp.maximum(late, flag_all[lax.rem(replica + DP - j, DP)][:1, :1])
     flag_ref[...] = jnp.broadcast_to(late, (8, 128))
 
-    @pl.loop(1, N)
-    def _(k):
-        ret_copy(me, peer(k)).wait_recv()
+    all_tables().wait_send()
+    for part in range(len(PARTS)):
+        all_vectors(part).wait_send()
+    for number in range(1, 4):
+        for copy in phase(number):
+            ag_copy(*copy).wait_send()
+    for j in range(1, DP):
+        flag_copy(j, replica).wait_send()
+
+    all_returns().wait_recv()
 
     total = jnp.zeros((2 * BOOKS, HOME), F32)
     for t in range(N // 2):
@@ -486,18 +501,7 @@
         total = total + dot(jnp.concatenate([high, low], axis=0), onehot)
     out_ref[...] = total[:BOOKS] + total[BOOKS:]
 
-    @pl.loop(1, N)
-    def _(k):
-        tab_copy(k, me).wait_send()
-        ret_copy(peer(k), me).wait_send()
-        for part in range(len(PARTS)):
-            vec_copy(part, k, peer(1), me).wait_send()
-
-    for number in range(1, 4):
-        for copy in phase(number):
-            ag_copy(*copy).wait_send()
-    for j in range(1, DP):
-        flag_copy(j, replica).wait_send()
+    all_returns().wait_send()
 
 
 def fast(embeddings, assign, list_slot, centroids, rotation, codebook):
@@ -533,10 +537,10 @@
             pltpu.VMEM((N, BOOKS, 128), F32),
             pltpu.VMEM((8, 128), I32),
             pltpu.VMEM((DP, 8, 128), I32),
-            dma((128,)), dma, dma, dma((len(PARTS),)),
-            dma((N,)), dma((N,)),
-            dma((len(PARTS), N)), dma((len(PARTS), N)),
-            dma((N,)), dma((N,)),
+            dma((2,)), dma, dma, dma((len(PARTS),)),
+            dma, dma,
+            dma((len(PARTS),)), dma((len(PARTS),)),
+            dma, dma,
             dma((14,)), dma((14,)),
             dma((DP,)), dma((DP,)),
         ],

time: 87.4 us -> 81.4 us (0.931)
  Pallas kernels: 84.7 us -> 78.7 us
    pallas_call x1, Pallas kernels: 84.7 us -> 78.7 us  [fast(): pl.pallas_call(kernel, out_shape=(jax.ShapeDtypeStruct((BOOKS, HOME), F32...]
where the time goes in v5:
time: 81.4 us; the launch traced here: 81.3 us
  Pallas kernels  78.7 us (97%)
  local copies, waits for them, and re-layouts  1.84 us (2%)
    pallas_call x1, Pallas kernels, fast(): pl.pallas_call(kernel, out_shape=(jax.ShapeDtypeStruct((BOOKS, HOME), F32...  78.7 us

profile of v5, /device:TPU:97, one launch (start us, length us, event | category | flops | bytes accessed | tf_op | source)
XLA Modules:
  0.0 81.3 jit_solution(14989265556684069398)
XLA Ops:
  0.0 0.0 copy-start.1
  0.0 0.0 copy-start.4
  0.0 0.0 copy-start
  0.0 0.0 copy-start.2
  0.0 78.7 %encode.1 = (f32[16,1024]{1,0:T(8,128)S(1)}, s32[8,128]{1,0:T(8,128)}) custom-call(bf16[32,32768]{1,0:T(8,128)(2,1)} %bitcast.64, s32[1,1024]{1,0:T(1,128)} %bitcast.80, s32[512,128]{1,0:T(8,128)} %bitcast.58, bf16[2048,1024]{1,0:T(8,128)(2,1)} %cent_ref.1, bf16[1024,1024]{1,0:T(8,128)(2,1)} %bitcast.69, bf16[16,64,256]{2,1,0:T(8,128)(2,1)} %bitcast.68), custom_call_target="tpu_custom_call" | custom-call | tf_op jit(solution)/shard_map/encode/pallas_call | solution.py:511
  78.7 1.2 %slice.9 = s32[1,1]{1,0:T(1,128)} slice(s32[8,128]{1,0:T(8,128)} %get-tuple-element.61), slice={[0:1], [0:1]} | slice | bytes 8 | tf_op jit(solution)/shard_map/slice | solution.py:626
  80.6 0.0 copy-done.1
  80.6 0.0 copy-done.4
  80.6 0.0 copy-done
  80.6 0.0 copy-done.2
  80.6 0.6 copy.63
  (1 shorter events, 0.0 us)
Async XLA Ops:
  0.0 80.6 %copy-start.1 = (bf16[32768,32]{0,1:T(8,128)(2,1)S(1)}, bf16[32768,32]{0,1:T(8,128)(2,1)}, u32[]{:S(2)}) copy-start(bf16[32768,32]{0,1:T(8,128)(2,1)} %param.10) | copy-start | bytes 6291460
  0.0 80.6 %copy-start.4 = (s32[1024]{0:T(1024)S(1)}, s32[1024]{0:T(1024)}, u32[]{:S(2)}) copy-start(s32[1024]{0:T(1024)} %param.11) | copy-start | bytes 12292
  0.0 80.6 %copy-start = (s32[65536]{0:T(1024)S(1)}, s32[65536]{0:T(1024)}, u32[]{:S(2)}) copy-start(s32[65536]{0:T(1024)} %param.12) | copy-start | bytes 786436
  0.0 80.6 %copy-start.2 = (bf16[16,256,64]{1,2,0:T(8,128)(2,1)S(1)}, bf16[16,256,64]{1,2,0:T(8,128)(2,1)}, u32[]{:S(2)}) copy-start(bf16[16,256,64]{1,2,0:T(8,128)(2,1)} %param.15) | copy-start | bytes 1572868

commit v6 on v5

--- a/solution.py
+++ b/solution.py
@@ -24,8 +24,8 @@
 FIRST = N * OVER
 SLOTS = FIRST + 128 * BLOCKS
 NEAR = 512
-GROUP = 4
-EARLY = 2
+GROUP = 8
+EARLY = 1
 PHASE = 2
 LATER = {1: 1, 2: 3}
 NEARS = -(-SLOTS // NEAR)
@@ -79,7 +79,7 @@
 def kernel(
     emb_ref, assign_ref, slots_ref, cent_ref, rot_ref, book_ref, out_ref, flag_ref,
     xb, send, recv, wide, near, cent, cent_t, rot, rot_t, codes, tab_own, tab_all, tab, tab_over, local_ref,
-    resid, sub, errs, code_ref, ret_send, ret_recv, flag_own, flag_all,
+    resid, sub, errs, code_ref, ret_send, ret_recv, arrive, flag_own, flag_all,
     x_sem, c_sem, r_sem, own_sem, tab_ss, tab_rs, vec_ss, vec_rs, ret_ss, ret_rs, ag_ss, ag_rs, flag_ss, flag_rs,
 ):
     me = lax.axis_index("lists")
@@ -158,7 +158,7 @@
     tab_all[me] = entry
     tab_all[N] = jnp.full((16, 128), NOBODY, I32)
     xb[BLOCKS - 1, 256:, :] = jnp.zeros((128, 256), BF16)
-    sub[:, SUB:, :] = jnp.ones((8, SUB, 1024), BF16)
+    sub[:, SUB:, :] = jnp.ones((16, SUB, 1024), BF16)
 
     @pl.loop(0, BOOKS)
     def _(m):
@@ -391,17 +391,17 @@
             start_phase(3)
 
     def encode(width, lanes):
-        @pl.loop(0, 2)
+        @pl.loop(0, 1)
         def _(i):
-            rows = pl.ds(pl.multiple_of(i * 512, 512), 512)
+            rows = pl.ds(pl.multiple_of(i * 1024, 1024), 1024)
             turned = dot(rot_t[rows, :], resid[:, :width]).astype(BF16)
-            for j in range(8):
+            for j in range(16):
                 piece = turned[SUB * j : SUB * (j + 1)]
                 sub[j, :SUB, :width] = piece
                 squares = piece.astype(F32)
                 length = jnp.sum(squares * squares, axis=0, keepdims=True)
-                least = jnp.min(dot(codes[8 * i + j], sub[j, :, :width]), axis=0, keepdims=True)
-                errs[pl.ds(8 * i + j, 1), lanes] = (length + least) * (1.0 / SUB)
+                least = jnp.min(dot(codes[16 * i + j], sub[j, :, :width]), axis=0, keepdims=True)
+                errs[pl.ds(16 * i + j, 1), lanes] = (length + least) * (1.0 / SUB)
 
     def minus(a, b):
         return (a.astype(F32) - b.astype(F32)).astype(BF16)
@@ -490,6 +490,9 @@
     for j in range(1, DP):
         flag_copy(j, replica).wait_send()
 
+    for t in range(N // 2):
+        arrive[t] = onehots(iota((256, HOME), 0) + 256 * t == code_ref[...])
+
     all_returns().wait_recv()
 
     total = jnp.zeros((2 * BOOKS, HOME), F32)
@@ -497,8 +500,7 @@
         got = jnp.concatenate([ret_recv[2 * t], ret_recv[2 * t + 1]], axis=1)
         high = got.astype(BF16)
         low = (got - high.astype(F32)).astype(BF16)
-        onehot = onehots(iota((256, HOME), 0) + 256 * t == code_ref[...])
-        total = total + dot(jnp.concatenate([high, low], axis=0), onehot)
+        total = total + dot(jnp.concatenate([high, low], axis=0), arrive[t])
     out_ref[...] = total[:BOOKS] + total[BOOKS:]
 
     all_returns().wait_send()
@@ -530,11 +532,12 @@
             pltpu.VMEM((N // 2, 128), I32),
             pltpu.VMEM((1, NEARS * NEAR), I32),
             pltpu.VMEM((D, 1024), BF16),
-            pltpu.VMEM((8, 2 * SUB, 1024), BF16),
+            pltpu.VMEM((16, 2 * SUB, 1024), BF16),
             pltpu.VMEM((BOOKS, SLOTS), F32),
             pltpu.VMEM((1, HOME), I32),
             pltpu.VMEM((N, BOOKS, 128), F32),
             pltpu.VMEM((N, BOOKS, 128), F32),
+            pltpu.VMEM((N // 2, 256, HOME), BF16),
             pltpu.VMEM((8, 128), I32),
             pltpu.VMEM((DP, 8, 128), I32),
             dma((2,)), dma, dma, dma((len(PARTS),)),

time: 81.4 us -> 80.1 us (0.984)
  Pallas kernels: 78.7 us -> 77.2 us
    pallas_call x1, Pallas kernels: 78.7 us -> 77.2 us  [fast(): pl.pallas_call(kernel, out_shape=(jax.ShapeDtypeStruct((BOOKS, HOME), F32...]
where the time goes in v6:
time: 80.1 us; the launch traced here: 80 us
  Pallas kernels  77.2 us (96%)
  local copies, waits for them, and re-layouts  1.84 us (2%)
    pallas_call x1, Pallas kernels, fast(): pl.pallas_call(kernel, out_shape=(jax.ShapeDtypeStruct((BOOKS, HOME), F32...  77.2 us

profile of v6, /device:TPU:97, one launch (start us, length us, event | category | flops | bytes accessed | tf_op | source)
XLA Modules:
  0.0 80.0 jit_solution(15403772149125807734)
XLA Ops:
  0.0 0.0 copy-start.1
  0.0 0.0 copy-start.4
  0.0 0.0 copy-start
  0.0 0.0 copy-start.2
  0.0 77.2 %encode.1 = (f32[16,1024]{1,0:T(8,128)S(1)}, s32[8,128]{1,0:T(8,128)}) custom-call(bf16[32,32768]{1,0:T(8,128)(2,1)} %bitcast.64, s32[1,1024]{1,0:T(1,128)} %bitcast.80, s32[512,128]{1,0:T(8,128)} %bitcast.58, bf16[2048,1024]{1,0:T(8,128)(2,1)} %cent_ref.1, bf16[1024,1024]{1,0:T(8,128)(2,1)} %bitcast.69, bf16[16,64,256]{2,1,0:T(8,128)(2,1)} %bitcast.68), custom_call_target="tpu_custom_call" | custom-call | tf_op jit(solution)/shard_map/encode/pallas_call | solution.py:513
  77.2 1.2 %slice.9 = s32[1,1]{1,0:T(1,128)} slice(s32[8,128]{1,0:T(8,128)} %get-tuple-element.61), slice={[0:1], [0:1]} | slice | bytes 8 | tf_op jit(solution)/shard_map/slice | solution.py:629
  79.1 0.0 copy-done.1
  79.1 0.0 copy-done.4
  79.1 0.0 copy-done
  79.1 0.0 copy-done.2
  79.1 0.3 conditional.1
  79.4 0.6 copy.63
Async XLA Ops:
  0.0 79.1 %copy-start.1 = (bf16[32768,32]{0,1:T(8,128)(2,1)S(1)}, bf16[32768,32]{0,1:T(8,128)(2,1)}, u32[]{:S(2)}) copy-start(bf16[32768,32]{0,1:T(8,128)(2,1)} %param.10) | copy-start | bytes 6291460
  0.0 79.1 %copy-start.4 = (s32[1024]{0:T(1024)S(1)}, s32[1024]{0:T(1024)}, u32[]{:S(2)}) copy-start(s32[1024]{0:T(1024)} %param.11) | copy-start | bytes 12292
  0.0 79.1 %copy-start = (s32[65536]{0:T(1024)S(1)}, s32[65536]{0:T(1024)}, u32[]{:S(2)}) copy-start(s32[65536]{0:T(1024)} %param.12) | copy-start | bytes 786436
  0.0 79.1 %copy-start.2 = (bf16[16,256,64]{1,2,0:T(8,128)(2,1)S(1)}, bf16[16,256,64]{1,2,0:T(8,128)(2,1)}, u32[]{:S(2)}) copy-start(bf16[16,256,64]{1,2,0:T(8,128)(2,1)} %param.15) | copy-start | bytes 1572868

commit v7 on v6

--- a/solution.py
+++ b/solution.py
@@ -432,11 +432,12 @@
             encode(1024, lanes)
 
     main_lanes = iota((BOOKS, 128), 1) < 64
-    def main(part):
-        low, high = PARTS[part]
-        own_copy(part).wait()
-
-        all_vectors(part).wait_recv()
+    def main(parts):
+        low, high = PARTS[parts[0]][0], PARTS[parts[-1]][1]
+        for part in parts:
+            own_copy(part).wait()
+            all_vectors(part).wait_recv()
+
 
         width, base = 128 * (high - low), FIRST + 128 * low
 
@@ -472,9 +473,10 @@
                 ret_copy(home, me).start()
 
     overflow()
-    for part in range(len(PARTS)):
-        main(part)
-        give_back(part)
+    for parts in ((0, 1), (2,)):
+        main(parts)
+        for part in parts:
+            give_back(part)
 
     for j in range(1, DP):
         flag_copy(j, lax.rem(replica + DP - j, DP)).wait_recv()

time: 80.1 us -> 80.8 us (level); the launches traced: 80 us -> 79.8 us
  no operation moved by 1% of the time
where the time goes in v7:
time: 80.8 us; the launch traced here: 79.8 us
  Pallas kernels  76.9 us (95%)
  local copies, waits for them, and re-layouts  1.84 us (2%)
    pallas_call x1, Pallas kernels, fast(): pl.pallas_call(kernel, out_shape=(jax.ShapeDtypeStruct((BOOKS, HOME), F32...  76.9 us

profile of v7, /device:TPU:97, one launch (start us, length us, event | category | flops | bytes accessed | tf_op | source)
XLA Modules:
  0.0 79.8 jit_solution(5331038704768335071)
XLA Ops:
  0.0 0.0 copy-start.1
  0.0 0.0 copy-start.4
  0.0 0.0 copy-start
  0.0 0.0 copy-start.2
  0.0 76.9 %encode.1 = (f32[16,1024]{1,0:T(8,128)S(1)}, s32[8,128]{1,0:T(8,128)}) custom-call(bf16[32,32768]{1,0:T(8,128)(2,1)} %bitcast.64, s32[1,1024]{1,0:T(1,128)} %bitcast.80, s32[512,128]{1,0:T(8,128)} %bitcast.58, bf16[2048,1024]{1,0:T(8,128)(2,1)} %cent_ref.1, bf16[1024,1024]{1,0:T(8,128)(2,1)} %bitcast.69, bf16[16,64,256]{2,1,0:T(8,128)(2,1)} %bitcast.68), custom_call_target="tpu_custom_call" | custom-call | tf_op jit(solution)/shard_map/encode/pallas_call | solution.py:515
  77.0 1.2 %slice.9 = s32[1,1]{1,0:T(1,128)} slice(s32[8,128]{1,0:T(8,128)} %get-tuple-element.61), slice={[0:1], [0:1]} | slice | bytes 8 | tf_op jit(solution)/shard_map/slice | solution.py:631
  78.8 0.0 copy-done.1
  78.8 0.0 copy-done.4
  78.8 0.0 copy-done
  78.8 0.0 copy-done.2
  78.9 0.3 conditional.1
  79.1 0.6 copy.63
Async XLA Ops:
  0.0 78.8 %copy-start.1 = (bf16[32768,32]{0,1:T(8,128)(2,1)S(1)}, bf16[32768,32]{0,1:T(8,128)(2,1)}, u32[]{:S(2)}) copy-start(bf16[32768,32]{0,1:T(8,128)(2,1)} %param.10) | copy-start | bytes 6291460
  0.0 78.8 %copy-start.4 = (s32[1024]{0:T(1024)S(1)}, s32[1024]{0:T(1024)}, u32[]{:S(2)}) copy-start(s32[1024]{0:T(1024)} %param.11) | copy-start | bytes 12292
  0.0 78.8 %copy-start = (s32[65536]{0:T(1024)S(1)}, s32[65536]{0:T(1024)}, u32[]{:S(2)}) copy-start(s32[65536]{0:T(1024)} %param.12) | copy-start | bytes 786436
  0.0 78.8 %copy-start.2 = (bf16[16,256,64]{1,2,0:T(8,128)(2,1)S(1)}, bf16[16,256,64]{1,2,0:T(8,128)(2,1)}, u32[]{:S(2)}) copy-start(bf16[16,256,64]{1,2,0:T(8,128)(2,1)} %param.15) | copy-start | bytes 1572868
